TPU v7x, 32 devices: a whole 2x2x4 slice. The times are simulated.
32 devices in a mesh: dp: 8 (over y, x, core), fsdp: 4 (over z).
Axes of the slice: x: 2, y: 2, z: 4, core: 2. Of those that a mesh axis runs over, the one named last changes fastest.
Arguments:
- tokens: bfloat16 [32768, 768], P(('dp', 'fsdp')), may hold values from -6 to 6
- qkv_weight: float32 [768, 2304], P('fsdp', 'dp'), may hold values from -0.21875 to 0.21875
- out_weight: float32 [768, 768], P('fsdp', 'dp'), may hold values from -2.5 to 2.5
- fc_weight: float32 [768, 3072], P('fsdp', 'dp'), may hold values from -0.21875 to 0.21875
- proj_weight: float32 [3072, 768], P('fsdp', 'dp'), may hold values from -0.109375 to 0.109375
- fc_bias: float32 [3072], P('dp'), may hold values from -1.2 to 1.2
- vectors: float32 [8, 768], P(None, 'dp'), may hold values from -0.8 to 1.4, as said below
- cotangent: bfloat16 [32768, 768], P(('dp', 'fsdp')), may hold values from -6 to 6
- lengths: int32 [32], P(('dp', 'fsdp')), may hold values from 64 to 1024, as said below
- clip_norm: float32 [], replicated, may hold values from 12000 to 24000
- noise_qkv: float32 [768, 2304], P('fsdp', 'dp'), may hold values from -4 to 4
- noise_out: float32 [768, 768], P('fsdp', 'dp'), may hold values from -4 to 4
- noise_fc: float32 [768, 3072], P('fsdp', 'dp'), may hold values from -4 to 4
- noise_proj: float32 [3072, 768], P('fsdp', 'dp'), may hold values from -4 to 4
- noise_fc_bias: float32 [3072], P('dp'), may hold values from -4 to 4
- noise_vectors: float32 [8, 768], P(None, 'dp'), may hold values from -4 to 4
Outputs:
- block_out: bfloat16 [32768, 768], P(('dp', 'fsdp'))
- input_grad: bfloat16 [32768, 768], P(('dp', 'fsdp'))
- norm_ratio: float32 [32], P(('dp', 'fsdp'))
- grad_qkv: float32 [768, 2304], P('fsdp', 'dp')
- grad_out: float32 [768, 768], P('fsdp', 'dp')
- grad_fc: float32 [768, 3072], P('fsdp', 'dp')
- grad_proj: float32 [3072, 768], P('fsdp', 'dp')
- grad_fc_bias: float32 [3072], P('dp')
- grad_vectors: float32 [8, 768], P(None, 'dp')
Inputs may be any that keep to these rules, and one draw needn't show every extreme that they name: `lengths`: each sequence's real length; at least one sequence has exactly 1024. `vectors`: gain rows near 1, bias rows of order a tenth.
All inputs are finite; a program needn't handle non-finite values.
Results may differ from a plain program's by a relative error of at most 0.014.
Values may be sent and summed in bfloat16 or wider, within the bound.
A program may use at most 320 MiB of HBM per device.

v0:
```python
import jax
import jax.numpy as jnp
from jax import lax
from jax.sharding import PartitionSpec as P

HD = 64


epsilon = 1e-05


def norm_layer(values, gain_row, shift_row):
    center = values - jnp.mean(values, axis=-1, keepdims=True)
    spread = jnp.mean(center * center, axis=-1, keepdims=True)
    return center * lax.rsqrt(spread + epsilon) * gain_row + shift_row


def gelu_tanh(values):
    return jax.nn.gelu(values, approximate=True)


def masked_scores(query_rows, key_rows, offset, length, scaling):
    scores = (
        jnp.einsum("qhd,khd->hqk", query_rows, key_rows, preferred_element_type=jnp.float32)
        * scaling
    )
    places = offset + jnp.arange(query_rows.shape[0], dtype=jnp.int32)
    key_places = jnp.arange(key_rows.shape[0], dtype=jnp.int32)
    allowed = (key_places[None, :] <= places[:, None]) & (key_places[None, :] < length)
    return jnp.where(allowed[None], scores, -1e30)


def attend(queries, key_rows, value_rows, length, block_rows, scaling):
    results = []
    log_parts = []
    for offset in range(0, queries.shape[0], block_rows):
        scores = masked_scores(
            queries[offset : offset + block_rows], key_rows, offset, length, scaling
        )
        row_peak = jnp.max(scores, axis=-1, keepdims=True)
        powers = jnp.exp(scores - row_peak)
        row_total = jnp.sum(powers, axis=-1, keepdims=True)
        chances = (powers / row_total).astype(jnp.bfloat16)
        results.append(
            jnp.einsum("hqk,khd->qhd", chances, value_rows, preferred_element_type=jnp.float32)
        )
        log_parts.append(row_peak + jnp.log(row_total))
    return (jnp.concatenate(results, axis=0), jnp.concatenate(log_parts, axis=1))


def attend_back(queries, key_rows, value_rows, grad_rows, log_sums, length, block_rows, scaling):
    grad_query = []
    grad_key = jnp.zeros(key_rows.shape, jnp.float32)
    grad_value = jnp.zeros(value_rows.shape, jnp.float32)
    for offset in range(0, queries.shape[0], block_rows):
        query_rows = queries[offset : offset + block_rows]
        scores = masked_scores(query_rows, key_rows, offset, length, scaling)
        chances = jnp.exp(scores - log_sums[:, offset : offset + block_rows])
        grad_block = grad_rows[offset : offset + block_rows]
        grad_value = grad_value + jnp.einsum(
            "hqk,qhd->khd",
            chances.astype(jnp.bfloat16),
            grad_block,
            preferred_element_type=jnp.float32,
        )
        grad_chances = jnp.einsum(
            "qhd,khd->hqk", grad_block, value_rows, preferred_element_type=jnp.float32
        )
        inner = jnp.sum(chances * grad_chances, axis=-1, keepdims=True)
        grad_scores = (chances * (grad_chances - inner)).astype(jnp.bfloat16)
        grad_query.append(
            jnp.einsum("hqk,khd->qhd", grad_scores, key_rows, preferred_element_type=jnp.float32)
            * scaling
        )
        grad_key = (
            grad_key
            + jnp.einsum(
                "hqk,qhd->khd", grad_scores, query_rows, preferred_element_type=jnp.float32
            )
            * scaling
        )
    return (jnp.concatenate(grad_query, axis=0), grad_key, grad_value)


def shards(
    tokens,
    qkv_weight,
    out_weight,
    fc_weight,
    proj_weight,
    fc_bias,
    vectors,
    cotangent,
    lengths,
    clip_norm,
    noise_qkv,
    noise_out,
    noise_fc,
    noise_proj,
    noise_fc_bias,
    noise_vectors,
):
    seq_count = lengths.shape[0]
    seq_len = tokens.shape[0] // seq_count
    width = tokens.shape[1]
    head_size = HD
    head_count = width // head_size
    block_rows = min(512, seq_len)
    scaling = head_size ** (-0.5)
    low_qkv = qkv_weight.astype(jnp.bfloat16)
    low_out = out_weight.astype(jnp.bfloat16)
    low_fc = fc_weight.astype(jnp.bfloat16)
    low_proj = proj_weight.astype(jnp.bfloat16)
    attn_cols = (
        lax.all_gather(low_qkv, "dp", axis=1, tiled=True),
        lax.all_gather(low_out, "dp", axis=1, tiled=True),
        lax.all_gather(vectors.astype(jnp.bfloat16), "dp", axis=1, tiled=True),
    )
    weight_qkv, weight_out = (
        lax.all_gather(attn_cols[0], "fsdp", axis=0, tiled=True),
        lax.all_gather(attn_cols[1], "fsdp", axis=0, tiled=True),
    )
    vector_rows = attn_cols[2].astype(jnp.float32)
    gain_one, shift_one, query_shift, value_shift = (
        vector_rows[0],
        vector_rows[1],
        vector_rows[2],
        vector_rows[3],
    )
    out_shift, gain_two, shift_two, proj_shift = (
        vector_rows[4],
        vector_rows[5],
        vector_rows[6],
        vector_rows[7],
    )
    qkv_shift = jnp.concatenate([query_shift, jnp.zeros_like(query_shift), value_shift])
    mlp_cols = (
        lax.all_gather(low_fc, "dp", axis=1, tiled=True),
        lax.all_gather(low_proj, "dp", axis=1, tiled=True),
        lax.all_gather(fc_bias.astype(jnp.bfloat16), "dp", axis=0, tiled=True),
    )
    weight_fc, weight_proj = (
        lax.all_gather(mlp_cols[0], "fsdp", axis=0, tiled=True),
        lax.all_gather(mlp_cols[1], "fsdp", axis=0, tiled=True),
    )
    fc_shift = mlp_cols[2].astype(jnp.float32)
    seq = 0
    inputs = tokens.astype(jnp.float32)
    length = lengths[seq]
    normed_one = norm_layer(inputs, gain_one, shift_one).astype(jnp.bfloat16)
    mixed = (
        jnp.dot(normed_one, weight_qkv, preferred_element_type=jnp.float32) + qkv_shift
    ).astype(jnp.bfloat16)
    heads_view = mixed.reshape(seq_len, 3, head_count, head_size)
    attended, log_sums = attend(
        heads_view[:, 0], heads_view[:, 1], heads_view[:, 2], length, block_rows, scaling
    )
    attended = attended.reshape(seq_len, width).astype(jnp.bfloat16)
    middle = inputs + jnp.dot(attended, weight_out, preferred_element_type=jnp.float32) + out_shift
    normed_two = norm_layer(middle, gain_two, shift_two).astype(jnp.bfloat16)
    hidden = jnp.dot(normed_two, weight_fc, preferred_element_type=jnp.float32) + fc_shift
    activated = gelu_tanh(hidden).astype(jnp.bfloat16)
    result = (
        middle + jnp.dot(activated, weight_proj, preferred_element_type=jnp.float32) + proj_shift
    )
    outputs = result.astype(jnp.bfloat16)
    saved = [
        (inputs, normed_one, heads_view, log_sums, attended, middle, normed_two, hidden, activated)
    ]
    back_mlp = (
        lax.all_gather(low_fc, "dp", axis=1, tiled=True),
        lax.all_gather(low_proj, "dp", axis=1, tiled=True),
    )
    back_fc, back_proj = (
        lax.all_gather(back_mlp[0], "fsdp", axis=0, tiled=True),
        lax.all_gather(back_mlp[1], "fsdp", axis=0, tiled=True),
    )
    back_attn = (
        lax.all_gather(low_qkv, "dp", axis=1, tiled=True),
        lax.all_gather(low_out, "dp", axis=1, tiled=True),
    )
    back_qkv, back_out = (
        lax.all_gather(back_attn[0], "fsdp", axis=0, tiled=True),
        lax.all_gather(back_attn[1], "fsdp", axis=0, tiled=True),
    )
    seq = 0
    inputs, normed_one, heads_view, log_sums, attended, middle, normed_two, hidden, activated = (
        saved[seq]
    )
    length = lengths[seq]
    real_rows = (jnp.arange(seq_len, dtype=jnp.int32) < length).astype(jnp.float32)[:, None]
    grad_y = cotangent.astype(jnp.float32) * real_rows
    grad_branch = grad_y.astype(jnp.bfloat16)
    grad_proj = jnp.dot(activated.T, grad_branch, preferred_element_type=jnp.float32)
    grad_pshift = jnp.sum(grad_branch.astype(jnp.float32), axis=0)
    grad_act = jnp.dot(grad_branch, back_proj.T, preferred_element_type=jnp.float32)
    gelu_out, gelu_pull = jax.vjp(gelu_tanh, hidden)
    grad_hidden = gelu_pull(grad_act)[0].astype(jnp.bfloat16)
    grad_fc = jnp.dot(normed_two.T, grad_hidden, preferred_element_type=jnp.float32)
    grad_fshift = jnp.sum(grad_hidden.astype(jnp.float32), axis=0)
    grad_normed_two = jnp.dot(grad_hidden, back_fc.T, preferred_element_type=jnp.float32)
    norm_out, second_pull = jax.vjp(norm_layer, middle, gain_two, shift_two)
    grad_mid, grad_gain_two, grad_shift_two = second_pull(grad_normed_two)
    grad_mid = grad_y + grad_mid
    grad_attn = grad_mid.astype(jnp.bfloat16)
    grad_out = jnp.dot(attended.T, grad_attn, preferred_element_type=jnp.float32)
    grad_oshift = jnp.sum(grad_attn.astype(jnp.float32), axis=0)
    grad_heads = jnp.dot(grad_attn, back_out.T, preferred_element_type=jnp.float32).astype(
        jnp.bfloat16
    )
    grad_heads = grad_heads.reshape(seq_len, head_count, head_size)
    grad_query, grad_key, grad_value = attend_back(
        heads_view[:, 0],
        heads_view[:, 1],
        heads_view[:, 2],
        grad_heads,
        log_sums,
        length,
        block_rows,
        scaling,
    )
    grad_mixed = (
        jnp.stack([grad_query, grad_key, grad_value], axis=1)
        .reshape(seq_len, 3 * width)
        .astype(jnp.bfloat16)
    )
    grad_qkv = jnp.dot(normed_one.T, grad_mixed, preferred_element_type=jnp.float32)
    grad_mshift = jnp.sum(grad_mixed.astype(jnp.float32), axis=0)
    grad_normed_one = jnp.dot(grad_mixed, back_qkv.T, preferred_element_type=jnp.float32)
    first_out, first_pull = jax.vjp(norm_layer, inputs, gain_one, shift_one)
    grad_in, grad_gain_one, grad_shift_one = first_pull(grad_normed_one)
    input_grads = (grad_mid + grad_in).astype(jnp.bfloat16)
    grad_vec = jnp.stack(
        [
            grad_gain_one,
            grad_shift_one,
            grad_mshift[:width],
            grad_mshift[2 * width :],
            grad_oshift,
            grad_gain_two,
            grad_shift_two,
            grad_pshift,
        ]
    )
    per_seq = (grad_qkv, grad_out, grad_fc, grad_proj, grad_fshift, grad_vec)
    squares = sum((jnp.sum(member * member) for member in per_seq))
    grad_norm = jnp.sqrt(squares)
    factor = jnp.minimum(1.0, clip_norm / grad_norm)
    ratios = [grad_norm / clip_norm]
    weighted = tuple((factor * member for member in per_seq))
    column_sums = (
        lax.psum_scatter(weighted[0], "dp", scatter_dimension=1, tiled=True),
        lax.psum_scatter(weighted[1], "dp", scatter_dimension=1, tiled=True),
        lax.psum_scatter(weighted[2], "dp", scatter_dimension=1, tiled=True),
        lax.psum_scatter(weighted[3], "dp", scatter_dimension=1, tiled=True),
        lax.psum_scatter(weighted[4], "dp", scatter_dimension=0, tiled=True),
        lax.psum_scatter(weighted[5], "dp", scatter_dimension=1, tiled=True),
    )
    row_sums = (
        lax.psum_scatter(
            column_sums[0].astype(jnp.bfloat16), "fsdp", scatter_dimension=0, tiled=True
        ).astype(jnp.float32),
        lax.psum_scatter(
            column_sums[1].astype(jnp.bfloat16), "fsdp", scatter_dimension=0, tiled=True
        ).astype(jnp.float32),
        lax.psum_scatter(
            column_sums[2].astype(jnp.bfloat16), "fsdp", scatter_dimension=0, tiled=True
        ).astype(jnp.float32),
        lax.psum_scatter(
            column_sums[3].astype(jnp.bfloat16), "fsdp", scatter_dimension=0, tiled=True
        ).astype(jnp.float32),
    )
    small_sums = lax.psum((column_sums[4], column_sums[5]), "fsdp")
    finals = (row_sums[0], row_sums[1], row_sums[2], row_sums[3], small_sums[0], small_sums[1])
    examples = lax.axis_size("dp") * lax.axis_size("fsdp") * seq_count
    return (
        outputs,
        input_grads,
        jnp.stack(ratios),
        finals[0] / examples + noise_qkv,
        finals[1] / examples + noise_out,
        finals[2] / examples + noise_fc,
        finals[3] / examples + noise_proj,
        finals[4] / examples + noise_fc_bias,
        finals[5] / examples + noise_vectors,
    )


def solution(mesh):
    placed = (
        P(("dp", "fsdp"), None),
        P("fsdp", "dp"),
        P("fsdp", "dp"),
        P("fsdp", "dp"),
        P("fsdp", "dp"),
        P("dp"),
        P(None, "dp"),
        P(("dp", "fsdp"), None),
        P(("dp", "fsdp")),
        P(),
        P("fsdp", "dp"),
        P("fsdp", "dp"),
        P("fsdp", "dp"),
        P("fsdp", "dp"),
        P("dp"),
        P(None, "dp"),
    )
    return jax.shard_map(
        shards,
        mesh=mesh,
        in_specs=placed,
        out_specs=(
            P(("dp", "fsdp"), None),
            P(("dp", "fsdp"), None),
            P(("dp", "fsdp")),
            P("fsdp", "dp"),
            P("fsdp", "dp"),
            P("fsdp", "dp"),
            P("fsdp", "dp"),
            P("dp"),
            P(None, "dp"),
        ),
        check_vma=False,
    )
```

profile of v0, /device:TPU:0, one launch (start us, length us, event | category | flops | bytes accessed | tf_op | source)
XLA Modules:
  0.0 985.4 jit_solution(14843088974218059995)
XLA Ops:
  11.9 14.5 %all_gather.39 = bf16[192,2304]{0,1:T(8,128)(2,1)S(1)} all-gather(bf16[192,288]{0,1:T(8,128)(2,1)S(1)} %copy.70), channel_id=1, replica_groups=mesh['dp'=8,'fsdp'=4] {'dp'}, dimensions={1}, use_global_device_ids=true | all-gather | bytes 995328 | tf_op jit(solution)/shard_map/all_gather | solution.py:115
  27.9 10.4 %all_gather.41 = bf16[192,768]{0,1:T(8,128)(2,1)S(1)} all-gather(bf16[192,96]{0,1:T(8,128)(2,1)S(1)} %copy.73), channel_id=1, replica_groups=mesh['dp'=8,'fsdp'=4] {'dp'}, dimensions={1}, use_global_device_ids=true | all-gather | bytes 331776 | tf_op jit(solution)/shard_map/all_gather | solution.py:116
  41.1 8.3 all-gather.1
  50.1 8.5 all-gather
  59.4 3.2 copy.76
  66.1 71.8 %all-gather.9.cloned.1.call-done = bf16[768,2304]{1,0:T(8,128)(2,1)} async-done(((bf16[192,2304]{1,0:T(8,128)(2,1)}), bf16[768,2304]{1,0:T(8,128)(2,1)}) %all-gather.9.cloned.1.call-update) | async-done | bytes 3538960 | tf_op jit(solution)/shard_map/all_gather | solution.py:120
  138.0 7.8 add_convert_fusion
  145.8 6.7 copy.72
  152.5 14.6 %fusion.20 = (f32[12,512]{1,0:T(8,128)S(1)}, f32[12,512,1024]{2,1,0:T(8,128)}) fusion(pred[512,1024]{1,0:T(8,128)(4,1)} %get-tuple-element.71, bf16[1024,3,12,64]{0,3,2,1:T(8,128)(2,1)} %bitcast.100), kind=kOutput, calls=%fused_computation.39 | convolution fusion | flops 824174592 | bytes 28073984 | tf_op jit(solution)/shard_map/qhd,khd->hqk/dot_general | solution.py:24
  167.1 13.0 %fusion.1 = f32[12,512]{1,0:T(8,128)S(1)} fusion(f32[12,512]{1,0:T(8,128)S(1)} %get-tuple-element.72, f32[12,512,1024]{2,1,0:T(8,128)} %get-tuple-element.73, pred[512,1024]{1,0:T(8,128)(4,1)} %get-tuple-element.71), kind=kLoop, calls=%fused_computation.13 | loop fusion | flops 25159680 | bytes 25739264 | tf_op jit(solution)/shard_map/reduce_sum | solution.py:42
  180.1 4.0 copy-done.1
  184.1 9.8 fusion.42
  193.9 11.4 %fusion.19 = (f32[12,512]{1,0:T(8,128)S(1)}, f32[12,512,1024]{2,1,0:T(8,128)}) fusion(pred[512,1024]{1,0:T(8,128)(4,1)S(1)} %get-tuple-element.70, bf16[1024,3,12,64]{0,3,2,1:T(8,128)(2,1)S(1)} %bitcast.104), kind=kOutput, calls=%fused_computation.38 | convolution fusion | flops 824174592 | bytes 28073984 | tf_op jit(solution)/shard_map/qhd,khd->hqk/dot_general | solution.py:24
  205.3 13.0 %fusion = f32[12,512]{1,0:T(8,128)} fusion(f32[12,512]{1,0:T(8,128)S(1)} %get-tuple-element.74, f32[12,512,1024]{2,1,0:T(8,128)} %get-tuple-element.75, pred[512,1024]{1,0:T(8,128)(4,1)S(1)} %get-tuple-element.70), kind=kLoop, calls=%fused_computation.12 | loop fusion | flops 25159680 | bytes 25739264 | tf_op jit(solution)/shard_map/reduce_sum | solution.py:42
  218.3 2.6 copy-done
  220.9 9.6 fusion.41
  230.5 2.7 pad_maximum_fusion
  233.2 3.8 fusion.72
  237.5 21.5 %all-gather.15.cloned.1.call-done = bf16[768,3072]{1,0:T(8,128)(2,1)} async-done(((bf16[192,3072]{1,0:T(8,128)(2,1)}), bf16[768,3072]{1,0:T(8,128)(2,1)}) %all-gather.15.cloned.1.call-update) | async-done | bytes 4718608 | tf_op jit(solution)/shard_map/all_gather | solution.py:143
  259.0 7.6 fusion.67
  266.6 4.8 copy-done.18
  271.3 11.3 %multiply_reduce_fusion.2 = (f32[]{:T(128)}, f32[3072,768]{1,0:T(8,128)}) fusion(bf16[1024,768]{0,1:T(8,128)(2,1)S(1)} %copy-done.11, f32[1024]{0:T(1024)S(1)} %copy-done.37, f32[1024,3072]{1,0:T(8,128)S(1)} %fusion.67, f32[3072]{0:T(1024)S(1)} %bitcast.129), kind=kOutput, calls=%fused_computation.35 | convolution fusion | flops 4870373376 | bytes 23609348 | tf_op jit(solution)/shard_map/dot_general | solution.py:194
  282.6 65.7 %all-gather.19.cloned.1.call-done = bf16[3072,768]{0,1:T(8,128)(2,1)} async-done(((bf16[768,768]{0,1:T(8,128)(2,1)}), bf16[3072,768]{0,1:T(8,128)(2,1)}) %all-gather.19.cloned.1.call-update) | async-done | bytes 4718608 | tf_op jit(solution)/shard_map/all_gather | solution.py:144
  348.3 17.6 %convert_reduce_fusion = (f32[3072]{0:T(1024)S(1)}, bf16[1024,3072]{1,0:T(8,128)(2,1)S(1)}) fusion(f32[1024,3072]{1,0:T(8,128)} %copy-done.18, f32[3072]{0:T(1024)S(1)} %bitcast.130, bf16[3072,768]{0,1:T(8,128)(2,1)} %all-gather.19.cloned.1.call-done, bf16[1024,768]{0,1:T(8,128)(2,1)} %copy.76, f32[1024]{0:T(1024)S(1)} %copy-done.37), kind=kOutput, calls=%fused_computation.27 | convolution fusion | flops 4906546176 | bytes 25194496 | tf_op jit(solution)/shard_map/dot_general | solution.py:196
  366.0 9.2 multiply_reduce_fusion.3
  375.1 9.0 fusion.74
  384.2 3.5 copy.77
  387.7 3.0 multiply_reduce_fusion.5
  394.3 3.5 multiply_reduce_fusion.8
  399.3 13.4 %fusion.11 = f32[12,64,1024]{2,1,0:T(8,128)} fusion(bf16[512,12,64]{0,2,1:T(8,128)(2,1)S(1)} %bitcast.119, f32[12,512]{1,0:T(8,128)S(1)} %log_add_fusion, f32[12,512,1024]{2,1,0:T(8,128)} %get-tuple-element.73, pred[512,1024]{1,0:T(8,128)(4,1)S(1)} %copy-done.17), kind=kOutput, calls=%fused_computation.25 | convolution fusion | flops 830472192 | bytes 29646848 | tf_op jit(solution)/shard_map/hqk,qhd->khd/dot_general | solution.py:60
  412.7 20.6 %multiply_reduce_fusion = (f32[12,512]{1,0:T(8,128)S(1)}, f32[12,512,1024]{2,1,0:T(8,128)}) fusion(f32[12,512]{1,0:T(8,128)S(1)} %log_add_fusion, f32[12,512,1024]{2,1,0:T(8,128)} %get-tuple-element.73, pred[512,1024]{1,0:T(8,128)(4,1)S(1)} %copy-done.17, bf16[512,12,64]{0,2,1:T(8,128)(2,1)S(1)} %bitcast.120, bf16[1024,3,12,64]{0,3,2,1:T(8,128)(2,1)} %bitcast.101), kind=kOutput, calls=%fused_computation.1 | convolution fusion | flops 836757504 | bytes 53264384 | tf_op jit(solution)/shard_map/qhd,khd->hqk/dot_general | solution.py:66
  433.3 20.2 %multiply_reduce_fusion.1 = (f32[12,512]{1,0:T(8,128)S(1)}, f32[12,512,1024]{2,1,0:T(8,128)}) fusion(f32[12,512]{1,0:T(8,128)S(1)} %log_add_fusion.1, f32[12,512,1024]{2,1,0:T(8,128)} %get-tuple-element.75, pred[512,1024]{1,0:T(8,128)(4,1)S(1)} %copy-done.15, bf16[512,12,64]{0,2,1:T(8,128)(2,1)S(1)} %bitcast.117, bf16[1024,3,12,64]{0,3,2,1:T(8,128)(2,1)} %bitcast.102), kind=kOutput, calls=%fused_computation.4 | convolution fusion | flops 836757504 | bytes 53264384 | tf_op jit(solution)/shard_map/qhd,khd->hqk/dot_general | solution.py:66
  453.5 42.5 %multiply_convert_fusion = (bf16[12,512,1024]{2,1,0:T(8,128)(2,1)}, bf16[12,512,1024]{2,1,0:T(8,128)(2,1)}) fusion(f32[12,512,1024]{2,1,0:T(8,128)} %get-tuple-element.81, f32[12,512]{1,0:T(8,128)S(1)} %get-tuple-element.80, f32[12,512]{1,0:T(8,128)S(1)} %log_add_fusion, f32[12,512,1024]{2,1,0:T(8,128)} %get-tuple-element.73, ...), kind=kLoop, calls=%fused_computation | loop fusion | flops 75497472 | bytes 126976000 | tf_op jit(solution)/shard_map/convert_element_type | solution.py:70
  496.0 9.5 multiply_bitcast_fusion.2
  505.5 7.1 fusion.50
  513.3 13.2 %add_bitcast_fusion = bf16[1024,1,12,64]{0,3,2,1:T(8,128)(2,1)} fusion(f32[12,64,1024]{2,1,0:T(8,128)S(1)} %copy-done.57, bf16[512,12,64]{0,2,1:T(8,128)(2,1)S(1)} %bitcast.118, f32[12,512]{1,0:T(8,128)S(1)} %log_add_fusion.1, f32[12,512,1024]{2,1,0:T(8,128)} %get-tuple-element.75, pred[512,1024]{1,0:T(8,128)(4,1)S(1)} %copy-done.16), kind=kOutput, calls=%fused_computation.66 | convolution fusion | flops 832045056 | bytes 31219712 | tf_op jit(solution)/shard_map/hqk,qhd->khd/dot_general | solution.py:60
  526.6 9.5 multiply_bitcast_fusion.1
  536.0 7.1 multiply_bitcast_fusion
  544.8 7.2 multiply_reduce_fusion.4
  552.1 5.5 fusion.73
  557.8 3.5 copy.78
  561.3 2.6 fusion.31
  570.1 3.3 broadcast_multiply_fusion.3
  573.3 3.0 copy.88
  576.4 6.4 broadcast_multiply_fusion.2
  582.8 8.2 copy.86
  591.1 7.8 broadcast_multiply_fusion
  599.0 9.7 copy.90
  608.7 9.1 broadcast_multiply_fusion.1
  620.8 66.1 %reduce-scatter.28.cloned.1.call-done = f32[288,768]{1,0:T(8,128)} async-done(((f32[2304,768]{1,0:T(8,128)}), f32[288,768]{1,0:T(8,128)}) %reduce-scatter.28.cloned.1.call-update) | async-done | bytes 884752
  686.9 2.2 copy.87
  690.6 76.3 %reduce-scatter.32.cloned.1.call-done = f32[96,3072]{1,0:T(8,128)} async-done(((f32[768,3072]{1,0:T(8,128)}), f32[96,3072]{1,0:T(8,128)}) %reduce-scatter.32.cloned.1.call-update) | async-done | bytes 1179664
  766.9 2.4 copy.91
  769.5 11.7 %add_convert_fusion.2 = bf16[1024,768]{0,1:T(8,128)(2,1)} fusion(f32[1024,768]{0,1:T(8,128)} %copy-done.5, bf16[3072,768]{0,1:T(8,128)(2,1)} %all-gather.19.cloned.1.call-done, f32[768]{0:T(1024)S(1)} %copy-done.47, f32[1024,3072]{1,0:T(8,128)} %copy-done.18, f32[3072]{0:T(1024)S(1)} %bitcast.131), kind=kOutput, calls=%fused_computation.72 | convolution fusion | flops 4865654784 | bytes 22035456 | tf_op jit(solution)/shard_map/dot_general | solution.py:164
  782.8 64.0 %reduce-scatter.22.cloned.1.call-done = f32[768,384]{1,0:T(8,128)} async-done(((f32[768,3072]{1,0:T(8,128)}), f32[768,384]{1,0:T(8,128)}) %reduce-scatter.22.cloned.1.call-update) | async-done | bytes 1179664 | tf_op jit(solution)/shard_map/reduce_scatter | solution.py:254
  846.8 2.2 convert_element_type.171
  849.8 2.6 copy.82
  853.9 23.0 %all-reduce = f32[3072]{0:T(1024)S(1)} all-reduce(f32[3072]{0:T(1024)S(1)} %broadcast_multiply_fusion.5), channel_id=10, replica_groups=mesh['dp'=8,'fsdp'=4] {'dp'}, use_global_device_ids=true, to_apply=%region_36.37.clone | all-reduce | flops 3072 | bytes 24576
  877.0 6.7 reduce-scatter.34.cloned.1.call-done
  884.6 11.9 %all-reduce.1 = (f32[384]{0:T(512)S(1)}, f32[8,96]{1,0:T(8,128)S(1)}) all-reduce(f32[384]{0:T(512)S(1)} %dynamic-slice.1, f32[8,96]{1,0:T(8,128)S(1)} %copy.93), channel_id=1, replica_groups=mesh['dp'=8,'fsdp'=4] {'fsdp'}, use_global_device_ids=true, to_apply=%region_37.38 | all-reduce | flops 1152 | bytes 9216 | tf_op jit(solution)/shard_map/psum | solution.py:273
  897.6 8.2 reduce-scatter.20.cloned.1.call-done
  907.2 21.2 %reduce-scatter.18.cloned.1.call-done = bf16[192,288]{1,0:T(8,128)(2,1)} async-done(((bf16[768,288]{1,0:T(8,128)(2,1)}), bf16[192,288]{1,0:T(8,128)(2,1)}) %reduce-scatter.18.cloned.1.call-update) | async-done | bytes 110608 | tf_op jit(solution)/shard_map/reduce_scatter | solution.py:260
  930.1 22.2 %reduce-scatter.26.cloned.1.call-done = bf16[768,96]{1,0:T(8,128)(2,1)} async-done(((bf16[3072,96]{1,0:T(8,128)(2,1)}), bf16[768,96]{1,0:T(8,128)(2,1)}) %reduce-scatter.26.cloned.1.call-update) | async-done | bytes 147472 | tf_op jit(solution)/shard_map/reduce_scatter | solution.py:269
  954.1 21.7 %reduce-scatter.24.cloned.1.call-done = bf16[192,384]{1,0:T(8,128)(2,1)} async-done(((bf16[768,384]{1,0:T(8,128)(2,1)}), bf16[192,384]{1,0:T(8,128)(2,1)}) %reduce-scatter.24.cloned.1.call-update) | async-done | bytes 147472 | tf_op jit(solution)/shard_map/reduce_scatter | solution.py:266
  (221 shorter events, 39.4 us)
Async XLA Ops:
  7.2 20.6 %copy-start.32 = (f32[192,96]{1,0:T(8,128)S(1)}, f32[192,96]{1,0:T(8,128)}, u32[]{:S(2)}) copy-start(f32[192,96]{1,0:T(8,128)} %param.18) | copy-start | bytes 221188
  7.2 33.9 %copy-start.53 = (f32[384]{0:T(512)S(1)}, f32[384]{0:T(512)}, u32[]{:S(2)}) copy-start(f32[384]{0:T(512)} %param.21) | copy-start | bytes 4612
  7.2 42.9 %copy-start.51 = (f32[8,96]{1,0:T(8,128)S(1)}, f32[8,96]{1,0:T(8,128)}, u32[]{:S(2)}) copy-start(f32[8,96]{1,0:T(8,128)} %param.22) | copy-start | bytes 9220
  7.2 51.4 %copy-start.23 = (bf16[1024,768]{1,0:T(8,128)(2,1)S(1)}, bf16[1024,768]{1,0:T(8,128)(2,1)}, u32[]{:S(2)}) copy-start(bf16[1024,768]{1,0:T(8,128)(2,1)} %param.16) | copy-start | bytes 4718596
  7.2 32.0 %all-gather.13.cloned.1.call-start = ((), (), s32[]{:S(2)}) async-start(), calls=%async_computation.11 | async-start | bytes 1327104 | tf_op jit(solution)/shard_map/all_gather | solution.py:138
  9.0 56.8 %all-gather.17.cloned.1.call-start = ((), (), s32[]{:S(2)}) async-start(), calls=%async_computation.13 | async-start | bytes 1327104 | tf_op jit(solution)/shard_map/all_gather | solution.py:139
  10.8 127.2 %all-gather.9.cloned.1.call-start = ((), (), s32[]{:S(2)}) async-start(), calls=%async_computation.9 | async-start | bytes 4423680 | tf_op jit(solution)/shard_map/all_gather | solution.py:120
  27.7 205.4 %all-gather.11.cloned.1.call-start = ((), (), s32[]{:S(2)}) async-start(), calls=%async_computation.10 | async-start | bytes 1474560 | tf_op jit(solution)/shard_map/all_gather | solution.py:121
  39.2 219.8 %all-gather.15.cloned.1.call-start = ((), (), s32[]{:S(2)}) async-start(), calls=%async_computation.12 | async-start | bytes 5898240 | tf_op jit(solution)/shard_map/all_gather | solution.py:143
  39.8 308.6 %all-gather.19.cloned.1.call-start = ((), (), s32[]{:S(2)}) async-start(), calls=%async_computation.14 | async-start | bytes 5898240 | tf_op jit(solution)/shard_map/all_gather | solution.py:144
  59.4 86.4 %copy-start.3 = (bf16[1024,768]{0,1:T(8,128)(2,1)}, bf16[1024,768]{0,1:T(8,128)(2,1)S(1)}, u32[]{:S(2)}) copy-start(bf16[1024,768]{0,1:T(8,128)(2,1)S(1)} %copy.68) | copy-start | bytes 4718596
  63.8 81.9 %copy-start.34 = (f32[768]{0:T(1024)}, f32[768]{0:T(1024)S(1)}, u32[]{:S(2)}) copy-start(f32[768]{0:T(1024)S(1)} %get-tuple-element.56) | copy-start | bytes 9220
  63.8 81.9 %copy-start.48 = (f32[768]{0:T(1024)}, f32[768]{0:T(1024)S(1)}, u32[]{:S(2)}) copy-start(f32[768]{0:T(1024)S(1)} %get-tuple-element.55) | copy-start | bytes 9220
  64.1 81.7 %copy-start.30 = (f32[1024]{0:T(1024)}, f32[1024]{0:T(1024)S(1)}, u32[]{:S(2)}) copy-start(f32[1024]{0:T(1024)S(1)} %broadcast_multiply_fusion.7) | copy-start | bytes 12292
  64.6 81.2 %copy-start.43 = (f32[1024]{0:T(1024)}, f32[1024]{0:T(1024)S(1)}, u32[]{:S(2)}) copy-start(f32[1024]{0:T(1024)S(1)} %fusion.30) | copy-start | bytes 12292
  64.6 81.2 %copy-start.39 = (f32[1024]{0:T(1024)}, f32[1024]{0:T(1024)S(1)}, u32[]{:S(2)}) copy-start(f32[1024]{0:T(1024)S(1)} %fusion.52) | copy-start | bytes 12292
  65.9 152.4 %copy-start.14 = (pred[512,1024]{1,0:T(8,128)(4,1)}, pred[512,1024]{1,0:T(8,128)(4,1)S(1)}, u32[]{:S(2)}) copy-start(pred[512,1024]{1,0:T(8,128)(4,1)S(1)} %get-tuple-element.70) | copy-start | bytes 1572868
  65.9 553.0 %reduce-scatter.30.cloned.1.call-start = ((), (), s32[]{:S(2)}) async-start(), calls=%async_computation.21 | async-start | bytes 2654208
  152.5 27.6 %copy-start.2 = (bf16[1024,2304]{0,1:T(8,128)(2,1)S(1)}, bf16[1024,2304]{0,1:T(8,128)(2,1)}, u32[]{:S(2)}) copy-start(bf16[1024,2304]{0,1:T(8,128)(2,1)} %copy.72) | copy-start | bytes 14155780
  167.1 17.1 %copy-start.1 = (f32[12,512,1024]{2,1,0:T(8,128)S(1)}, f32[12,512,1024]{2,1,0:T(8,128)}, u32[]{:S(2)}) copy-start(f32[12,512,1024]{2,1,0:T(8,128)} %get-tuple-element.73) | copy-start | bytes 75497472
  205.3 15.6 %copy-start = (f32[12,512,1024]{2,1,0:T(8,128)S(1)}, f32[12,512,1024]{2,1,0:T(8,128)}, u32[]{:S(2)}) copy-start(f32[12,512,1024]{2,1,0:T(8,128)} %get-tuple-element.75) | copy-start | bytes 75497472
  233.2 4.3 copy-start.29
  237.0 153.7 %copy-start.5 = (f32[1024,768]{0,1:T(8,128)}, f32[1024,768]{0,1:T(8,128)S(1)}, u32[]{:S(2)}) copy-start(f32[1024,768]{0,1:T(8,128)S(1)} %get-tuple-element.77) | copy-start | bytes 9437188
  259.0 12.3 %copy-start.11 = (bf16[1024,768]{0,1:T(8,128)(2,1)S(1)}, bf16[1024,768]{0,1:T(8,128)(2,1)}, u32[]{:S(2)}) copy-start(bf16[1024,768]{0,1:T(8,128)(2,1)} %copy.76) | copy-start | bytes 4718596
  259.0 12.3 %copy-start.37 = (f32[1024]{0:T(1024)S(1)}, f32[1024]{0:T(1024)}, u32[]{:S(2)}) copy-start(f32[1024]{0:T(1024)} %fusion.54) | copy-start | bytes 12292
  259.0 12.3 %copy-start.45 = (f32[8,1,384]{2,1,0:T(1,128)S(1)}, f32[8,1,384]{2,1,0:T(1,128)}, u32[]{:S(2)}) copy-start(f32[8,1,384]{2,1,0:T(1,128)} %convert_element_type.176) | copy-start | bytes 36868
  266.6 4.8 copy-start.18
  366.0 146.6 %copy-start.36 = (f32[3072]{0:T(1024)}, f32[3072]{0:T(1024)S(1)}, u32[]{:S(2)}) copy-start(f32[3072]{0:T(1024)S(1)} %get-tuple-element.90) | copy-start | bytes 36868
  391.6 6.2 copy-start.8
  391.6 6.1 copy-start.41
  399.3 34.0 %copy-start.21 = (bf16[512,768]{0,1:T(8,128)(2,1)}, bf16[512,768]{0,1:T(8,128)(2,1)S(1)}, u32[]{:S(2)}) copy-start(bf16[512,768]{0,1:T(8,128)(2,1)S(1)} %get-tuple-element.66) | copy-start | bytes 2359300
  412.7 20.6 %copy-start.15 = (pred[512,1024]{1,0:T(8,128)(4,1)S(1)}, pred[512,1024]{1,0:T(8,128)(4,1)}, u32[]{:S(2)}) copy-start(pred[512,1024]{1,0:T(8,128)(4,1)} %copy-done.14) | copy-start | bytes 1572868
  433.3 62.7 %slice-start = ((s8[4718592]{0:T(1024)(128)(4,1)}), s8[524288]{0:T(1024)(128)(4,1)S(1)}, s32[]{:S(2)}) async-start(s8[4718592]{0:T(1024)(128)(4,1)} %bitcast.106), calls=%async_computation.24 | async-start | bytes 1048576
  453.5 42.5 %slice-start.1 = ((s8[4718592]{0:T(1024)(128)(4,1)}), s8[4194304]{0:T(1024)(128)(4,1)S(1)}, s32[]{:S(2)}) async-start(s8[4718592]{0:T(1024)(128)(4,1)} %bitcast.106), calls=%async_computation.25 | async-start | bytes 8388608
  505.5 7.8 copy-start.16
  505.5 7.8 copy-start.22
  505.5 7.8 copy-start.57
  536.0 7.1 copy-start.19
  536.0 7.2 copy-start.20
  536.0 7.4 copy-start.25
  544.8 7.2 copy-start.54
  557.8 6.1 copy-start.44
  576.4 110.5 %reduce-scatter.28.cloned.1.call-start = ((), (), s32[]{:S(2)}) async-start(), calls=%async_computation.20 | async-start | bytes 7962624
  591.1 175.8 %reduce-scatter.32.cloned.1.call-start = ((), (), s32[]{:S(2)}) async-start(), calls=%async_computation.22 | async-start | bytes 10616832
  608.7 238.1 %reduce-scatter.22.cloned.1.call-start = ((), (), s32[]{:S(2)}) async-start(), calls=%async_computation.17 | async-start | bytes 10616832 | tf_op jit(solution)/shard_map/reduce_scatter | solution.py:254
  617.8 71.4 %copy-start.26 = (f32[768,96]{0,1:T(8,128)S(1)}, f32[768,96]{0,1:T(8,128)}, u32[]{:S(2)}) copy-start(f32[768,96]{0,1:T(8,128)} %param.29) | copy-start | bytes 884740
  617.8 71.6 %copy-start.56 = (u32[32]{0:T(128)S(1)}, u32[32]{0:T(128)}, u32[]{:S(2)}) copy-start(u32[32]{0:T(128)} %constant.56) | copy-start | bytes 388
  617.8 151.6 %copy-start.46 = (f32[8,1,384]{2,1,0:T(1,128)S(1)}, f32[8,1,384]{2,1,0:T(1,128)}, u32[]{:S(2)}) copy-start(f32[8,1,384]{2,1,0:T(1,128)} %convert_element_type.176) | copy-start | bytes 36868
  617.8 151.6 %copy-start.47 = (f32[768]{0:T(1024)S(1)}, f32[768]{0:T(1024)}, u32[]{:S(2)}) copy-start(f32[768]{0:T(1024)} %get-tuple-element.50) | copy-start | bytes 9220
  617.8 265.9 %reduce-scatter.34.cloned.1.call-start = ((), (), s32[]{:S(2)}) async-start(), calls=%async_computation.23 | async-start | bytes 442368
  618.9 286.9 %reduce-scatter.20.cloned.1.call-start = ((), (), s32[]{:S(2)}) async-start(), calls=%async_computation.16 | async-start | bytes 245760 | tf_op jit(solution)/shard_map/reduce_scatter | solution.py:263
  620.7 307.7 %reduce-scatter.18.cloned.1.call-start = ((), (), s32[]{:S(2)}) async-start(), calls=%async_computation.15 | async-start | bytes 737280 | tf_op jit(solution)/shard_map/reduce_scatter | solution.py:260
  689.1 263.2 %reduce-scatter.26.cloned.1.call-start = ((), (), s32[]{:S(2)}) async-start(), calls=%async_computation.19 | async-start | bytes 983040 | tf_op jit(solution)/shard_map/reduce_scatter | solution.py:269
  769.4 206.5 %reduce-scatter.24.cloned.1.call-start = ((), (), s32[]{:S(2)}) async-start(), calls=%async_computation.18 | async-start | bytes 737280 | tf_op jit(solution)/shard_map/reduce_scatter | solution.py:266
  769.4 11.7 %copy-start.7 = (f32[1024,768]{0,1:T(8,128)S(1)}, f32[1024,768]{0,1:T(8,128)}, u32[]{:S(2)}) copy-start(f32[1024,768]{0,1:T(8,128)} %copy.78) | copy-start | bytes 9437188
  769.4 11.7 %copy-start.9 = (f32[1024,768]{0,1:T(8,128)S(1)}, f32[1024,768]{0,1:T(8,128)}, u32[]{:S(2)}) copy-start(f32[1024,768]{0,1:T(8,128)} %copy-done.8) | copy-start | bytes 9437188
  769.5 11.7 %copy-start.13 = (bf16[1024,768]{0,1:T(8,128)(2,1)S(1)}, bf16[1024,768]{0,1:T(8,128)(2,1)}, u32[]{:S(2)}) copy-start(bf16[1024,768]{0,1:T(8,128)(2,1)} %copy.76) | copy-start | bytes 4718596
  769.5 11.7 %copy-start.38 = (f32[1024]{0:T(1024)S(1)}, f32[1024]{0:T(1024)}, u32[]{:S(2)}) copy-start(f32[1024]{0:T(1024)} %fusion.54) | copy-start | bytes 12292
  769.5 11.7 %copy-start.42 = (f32[1024]{0:T(1024)S(1)}, f32[1024]{0:T(1024)}, u32[]{:S(2)}) copy-start(f32[1024]{0:T(1024)} %copy-done.41) | copy-start | bytes 12292
  782.8 113.7 %copy-start.52 = (f32[384]{0:T(512)S(1)}, f32[384]{0:T(512)}, u32[]{:S(2)}) copy-start(f32[384]{0:T(512)} %param.30) | copy-start | bytes 4612
  782.8 114.2 %copy-start.50 = (f32[8,96]{1,0:T(8,128)S(1)}, f32[8,96]{1,0:T(8,128)}, u32[]{:S(2)}) copy-start(f32[8,96]{1,0:T(8,128)} %param.31) | copy-start | bytes 9220
  782.8 123.0 %copy-start.33 = (f32[192,96]{1,0:T(8,128)S(1)}, f32[192,96]{1,0:T(8,128)}, u32[]{:S(2)}) copy-start(f32[192,96]{1,0:T(8,128)} %param.27) | copy-start | bytes 221188
  782.8 145.6 %copy-start.27 = (f32[192,288]{1,0:T(8,128)S(1)}, f32[192,288]{1,0:T(8,128)}, u32[]{:S(2)}) copy-start(f32[192,288]{1,0:T(8,128)} %param.26) | copy-start | bytes 663556
  848.9 126.9 %copy-start.28 = (f32[192,384]{1,0:T(8,128)S(1)}, f32[192,384]{1,0:T(8,128)}, u32[]{:S(2)}) copy-start(f32[192,384]{1,0:T(8,128)} %param.28) | copy-start | bytes 884740
  (11 other events, 21.9 us)
Sparse Core Ops, SparseCore 0:
  10.5 28.6 all-gather.12
  41.7 24.0 all-gather.16
  67.9 69.9 all-gather.8
  140.0 29.0 all-gather.10
  170.4 88.5 all-gather.14
  260.4 87.8 all-gather.18
  576.5 40.8 reduce-scatter.29
  621.4 65.4 reduce-scatter.27
  690.4 76.4 reduce-scatter.31
  770.3 76.4 reduce-scatter.21
  849.8 33.8 reduce-scatter.33
  886.4 19.3 reduce-scatter.19
  908.2 20.2 reduce-scatter.17
  930.7 21.5 reduce-scatter.25
  954.5 21.2 reduce-scatter.23
where the time goes:
time: 991 us; the launch traced here: 985 us
  waiting for transfers between devices  446 us (45%)
  matrix products  241 us (24%)
  other arithmetic  127 us (13%)
  blocking collectives  76.6 us (8%)
  local copies, waits for them, and re-layouts  71.3 us (7%)
  between operations  22.1 us (2%)
    unnamed x19, waiting for transfers between devices  150 us
    all_gather x1, waiting for transfers between devices, shards(): lax.all_gather(attn_cols[0], 'fsdp', axis=0, tiled=True)  71.8 us
    all_gather x1, waiting for transfers between devices, shards(): lax.all_gather(mlp_cols[1], 'fsdp', axis=0, tiled=True)  65.7 us
    reduce_scatter x1, waiting for transfers between devices, shards(): lax.psum_scatter(weighted[2], 'dp', scatter_dimension=1, tiled=True)  64 us
    unnamed x139, local copies, waits for them, and re-layouts  54.3 us
    convert_element_type x1, other arithmetic, attend_back(): grad_scores = (chances * (grad_chances - inner)).astype(jnp.bfloat16)  42.5 us
    dot_general x2, matrix products, attend_back(): jnp.einsum('qhd,khd->hqk', grad_block, value_rows, preferred_element_type...  40.8 us
    mul x6, other arithmetic, shards(): weighted = tuple((factor * member for member in per_seq))  27.3 us
  transfers between devices with their start and end apart: 15, of which 11 were waited for; matrix products, arithmetic and copies ran while one was open for 20% of the time, Pallas kernels for 0%

commit v1 on v0

--- a/solution.py
+++ b/solution.py
@@ -1,7 +1,257 @@
-import jax
-import jax.numpy as jnp
+import jax, jax.numpy as jnp
 from jax import lax
-from jax.sharding import PartitionSpec as P
+from jax.experimental import pallas as pl
+from jax.experimental.pallas import tpu as pltpu
+P = jax.sharding.PartitionSpec
+MESH = pl.DeviceIdType.MESH
+bf16=jnp.bfloat16; f32=jnp.float32
+
+def place():
+    d = lax.axis_index("dp"); z = lax.axis_index("fsdp")
+    core = d % 2; xx = (d // 2) % 2; yy = d // 4
+    return d, z, d + 1 - 2*core, d + 2 - 4*xx, d + 4 - 8*yy
+
+def greet(partners):
+    bar = pltpu.get_barrier_semaphore()
+    for dev in partners:
+        pl.semaphore_signal(bar, inc=1, device_id=dev, device_id_type=MESH)
+    pl.semaphore_wait(bar, len(partners))
+
+class Gather:
+    def __init__(self, shards, zq, zo, full, send, recv):
+        self.sh = shards; self.zb = (zq, zo); self.full = full
+        self.send = send; self.recv = recv
+        self.d, self.z, self.sib, self.xn, self.yn = place()
+        self.dg = self.xn + self.yn - self.d
+        self.nz = lax.axis_size("fsdp")
+    def cp(self, src, dst, w, slot, dev):
+        return pltpu.make_async_remote_copy(src_ref=src, dst_ref=dst, send_sem=self.send.at[w, slot], recv_sem=self.recv.at[w, slot], device_id=dev, device_id_type=MESH)
+    def block(self, w, d, half=None):
+        ref = self.full[w]
+        if w == 4:
+            return ref.at[d] if half is None else ref.at[d, pl.ds(half * 8, 8)]
+        if w == 2:
+            cols = ref.shape[1] // 8
+            cs = pl.ds(pl.multiple_of(d * cols, 128), cols)
+            n = ref.shape[0]
+            rs = pl.ds(0, n) if half is None else pl.ds(half * (n // 2), n // 2)
+            return ref.at[rs, cs]
+        rows = ref.shape[0] // 8
+        if half is None:
+            return ref.at[pl.ds(pl.multiple_of(d * rows, 16), rows), :]
+        return ref.at[pl.ds(pl.multiple_of(d * rows + half * (rows // 2), 16), rows // 2), :]
+    def zslot(self, w, z):
+        if w < 2:
+            return self.zb[w].at[z]
+        ref = self.full[w]
+        if w == 2:
+            r, c = ref.shape[0] // self.nz, ref.shape[1] // 8
+            return ref.at[pl.ds(pl.multiple_of(z * r, 16), r), pl.ds(pl.multiple_of(self.d * c, 128), c)]
+        r, c = ref.shape[0] // 8, ref.shape[1] // self.nz
+        return ref.at[pl.ds(pl.multiple_of(self.d * r, 16), r), pl.ds(pl.multiple_of(z * c, 128), c)]
+    def partners(self):
+        return [(self.d, (self.z + j) % self.nz) for j in range(1, self.nz)] + [(self.sib, self.z), (self.xn, self.z), (self.yn, self.z)]
+    def zc(self, w, j, recv=False):
+        other = (self.z - j + self.nz) % self.nz if recv else (self.z + j) % self.nz
+        src = self.sh[w]
+        dst = self.zslot(w, other if recv else self.z)
+        return self.cp(src, dst, w, j - 1, (self.d, other))
+    def start(self, w):
+        if w == 4:
+            self.block(w, self.d)[...] = self.sh[w][...]
+            return
+        for j in range(1, self.nz):
+            self.zc(w, j).start()
+        self.zslot(w, self.z)[...] = self.sh[w][...]
+    def sibc(self, w, i, d):
+        return self.cp(self.block(w, d), self.block(w, d), w, 7 + i, (self.sib, self.z))
+    def bx(self, w, b, dev, slot, half=None):
+        return self.cp(self.block(w, b, half), self.block(w, b, half), w, slot, (dev, self.z))
+    def e1(self, w):
+        if w < 4:
+            for j in range(1, self.nz):
+                self.zc(w, j, True).wait_recv()
+        if w < 2:
+            self.block(w, self.d)[...] = jnp.concatenate([self.zb[w][k] for k in range(self.nz)], axis=1)
+        self.bx(w, self.d, self.xn, 3).start()
+        self.bx(w, self.d, self.yn, 4).start()
+        self.sibc(w, 0, self.d).start()
+    def e2(self, w):
+        self.bx(w, self.xn, self.xn, 3).wait_recv()
+        self.bx(w, self.xn, self.yn, 5, 0).start()
+        self.sibc(w, 1, self.xn).start()
+    def e3(self, w):
+        self.bx(w, self.yn, self.yn, 4).wait_recv()
+        self.bx(w, self.yn, self.xn, 6, 1).start()
+        self.sibc(w, 2, self.yn).start()
+    def e4(self, w):
+        self.bx(w, self.dg, self.yn, 5, 0).wait_recv()
+        self.bx(w, self.dg, self.xn, 6, 1).wait_recv()
+        self.sibc(w, 3, self.dg).start()
+    def e5(self, w):
+        o = self.sib - self.d
+        for i, b in enumerate((self.d, self.xn, self.yn, self.dg)):
+            self.sibc(w, i, b + o).wait_recv()
+    def finish(self, w):
+        if w < 4:
+            for j in range(1, self.nz):
+                self.zc(w, j).wait_send()
+        self.bx(w, self.d, self.xn, 3).wait_send()
+        self.bx(w, self.d, self.yn, 4).wait_send()
+        self.bx(w, self.xn, self.yn, 5, 0).wait_send()
+        self.bx(w, self.yn, self.xn, 6, 1).wait_send()
+        for i, b in enumerate((self.d, self.xn, self.yn, self.dg)):
+            self.sibc(w, i, b).wait_send()
+
+def ag_kernel(sq, so, sf, sp, sv, QT, OT, F, PT, V, zq, zo, send, recv):
+    g = Gather((sq, so, sf, sp, sv), zq, zo, (QT, OT, F, PT, V), send, recv)
+    greet(g.partners())
+    for w in (4, 0, 1, 2, 3): g.start(w)
+    g.e1(4); g.e2(4); g.e3(4); g.e4(4)
+    g.e1(0); g.e1(1); g.e2(0); g.e3(0); g.e1(2); g.e2(1); g.e3(1); g.e4(0); g.e4(1); g.e1(3)
+    g.e2(2); g.e3(2); g.e4(2); g.e2(3); g.e3(3); g.e4(3)
+    for w in range(5): g.e5(w)
+    for w in range(5): g.finish(w)
+
+def gather_all(sq, so, sf, sp, sv):
+    ndp, nz = lax.axis_size("dp"), lax.axis_size("fsdp")
+    D = sq.shape[1] * nz
+    shapes = [(sq.shape[0]*ndp, D), (so.shape[0]*ndp, D), (D, sf.shape[1]*ndp), (sp.shape[0]*ndp, sp.shape[1]*nz)]
+    vm = pl.BlockSpec(memory_space=pltpu.VMEM)
+    return pl.pallas_call(ag_kernel, out_shape=[jax.ShapeDtypeStruct(s, bf16) for s in shapes] + [jax.ShapeDtypeStruct((ndp,) + sv.shape, f32)],
+        in_specs=[vm]*5, out_specs=[vm]*5,
+        scratch_shapes=[pltpu.VMEM((nz,)+sq.shape, bf16), pltpu.VMEM((nz,)+so.shape, bf16),
+            pltpu.SemaphoreType.DMA((5, 11)), pltpu.SemaphoreType.DMA((5, 11))],
+        compiler_params=pltpu.CompilerParams(collective_id=0, has_side_effects=True, vmem_limit_bytes=60<<20))(sq, so, sf, sp, sv)
+
+class Scatter:
+    def __init__(self, grads, sibs, ras, rbs, rxs, rys, zss, zrs, outs, cs, csend, crecv, send, recv):
+        self.g = grads; self.sb = sibs; self.ra = ras; self.rb = rbs; self.rx = rxs; self.ry = rys
+        self.zs = zss; self.zr = zrs; self.out = outs; self.send = send; self.recv = recv
+        self.cs = cs; self.csend = csend; self.crecv = crecv
+        self.d, self.z, self.sib, self.xn, self.yn = place()
+        self.dg = self.xn + self.yn - self.d
+        self.nz = lax.axis_size("fsdp")
+    def partners(self):
+        return [(self.d, (self.z + j) % self.nz) for j in range(1, self.nz)] + [(self.sib, self.z), (self.xn, self.z), (self.yn, self.z)]
+    def cp(self, src, dst, w, slot, dev):
+        return pltpu.make_async_remote_copy(src_ref=src, dst_ref=dst, send_sem=self.send.at[w, slot], recv_sem=self.recv.at[w, slot], device_id=dev, device_id_type=MESH)
+    def block(self, w, d):
+        ref = self.g[w]
+        if w == 4:
+            return ref.at[d]
+        if w == 2:
+            cols = ref.shape[1] // 8
+            return ref.at[:, pl.ds(pl.multiple_of(d * cols, 128), cols)]
+        rows = ref.shape[0] // 8
+        return ref.at[pl.ds(pl.multiple_of(d * rows, 16), rows), :]
+    def half(self, ref, h):
+        n = ref.shape[0] // 2
+        return ref.at[pl.ds(h * n, n)]
+    def chips(self): return (self.dg, self.xn, self.yn, self.d)
+    def sibc(self, w, i):
+        o = self.sib - self.d
+        return self.cp(self.block(w, self.chips()[i] + o), self.sb[w].at[i], w, i, (self.sib, self.z))
+    def start_c(self, c):
+        self.cs[0] = jnp.full((8, 128), c, f32)
+        self.cc().start()
+    def cc(self):
+        return pltpu.make_async_remote_copy(src_ref=self.cs.at[0], dst_ref=self.cs.at[1], send_sem=self.csend, recv_sem=self.crecv, device_id=(self.sib, self.z), device_id_type=MESH)
+    def s0(self, w):
+        for i in range(4): self.sibc(w, i).start()
+    def hsend(self, w, i, h, slot, dev, dst):
+        return self.cp(self.half(self.sb[w].at[i], h), dst, w, slot, (dev, self.z))
+    def ca(self, w): return self.hsend(w, 0, 0, 4, self.xn, self.ra[w])
+    def cb(self, w): return self.hsend(w, 0, 1, 5, self.yn, self.rb[w])
+    def cx(self, w, h): return self.hsend(w, 1, h, 6 + h, self.xn, self.half(self.rx[w], h))
+    def cy(self, w, h): return self.hsend(w, 2, h, 8 + h, self.yn, self.half(self.ry[w], h))
+    def mix(self, w, i):
+        c0 = self.cs[0, 0:1, 0:1]; c1 = self.cs[1, 0:1, 0:1]
+        ref = self.sb[w].at[i]
+        ref[...] = (c0 * self.block(w, self.chips()[i])[...].astype(f32) + c1 * ref[...].astype(f32)).astype(ref.dtype)
+    def a(self, w):
+        self.sibc(w, 0).wait_recv(); self.mix(w, 0); self.ca(w).start(); self.cb(w).start()
+        self.sibc(w, 1).wait_recv(); self.mix(w, 1); self.cx(w, 0).start()
+        self.sibc(w, 2).wait_recv(); self.mix(w, 2); self.cy(w, 1).start()
+    def r(self, w):
+        self.ca(w).wait_recv()
+        ref = self.half(self.sb[w].at[2], 0)
+        ref[...] = (ref[...].astype(f32) + self.ra[w][...].astype(f32)).astype(ref.dtype)
+        self.cy(w, 0).start()
+        self.cb(w).wait_recv()
+        ref = self.half(self.sb[w].at[1], 1)
+        ref[...] = (ref[...].astype(f32) + self.rb[w][...].astype(f32)).astype(ref.dtype)
+        self.cx(w, 1).start()
+    def zpiece(self, w, k):
+        if w in (0, 1): return self.zs[w].at[k]
+        own = self.zs[w]
+        if w == 4: return own
+        if w == 2:
+            r = own.shape[0] // self.nz
+            return own.at[pl.ds(pl.multiple_of(k * r, 16), r)]
+        c = own.shape[1] // self.nz
+        return own.at[:, pl.ds(pl.multiple_of(k * c, 128), c)]
+    def zc(self, w, j):
+        to = (self.z + j) % self.nz
+        return self.cp(self.zpiece(w, to), self.zr[w].at[j - 1], w, 9 + j, (self.d, to))
+    def f(self, w):
+        self.sibc(w, 3).wait_recv()
+        for h in (0, 1):
+            self.cx(w, h).wait_recv(); self.cy(w, h).wait_recv()
+        c0 = self.cs[0, 0:1, 0:1]; c1 = self.cs[1, 0:1, 0:1]
+        t = c0 * self.block(w, self.d)[...].astype(f32) + c1 * self.sb[w][3].astype(f32)
+        t = t + self.rx[w][...].astype(f32) + self.ry[w][...].astype(f32)
+        if w in (0, 1):
+            c = t.shape[1] // self.nz
+            for k in range(self.nz): self.zs[w][k] = t[:, k * c:(k + 1) * c].astype(bf16)
+        else:
+            self.zs[w][...] = t.astype(self.zs[w].dtype)
+        for j in range(1, self.nz): self.zc(w, j).start()
+    def zf(self, w):
+        for j in range(1, self.nz): self.zc(w, j).wait_recv()
+        t = self.zpiece(w, self.z)[...].astype(f32)
+        for j in range(self.nz - 1): t = t + self.zr[w][j].astype(f32)
+        self.out[w][...] = t
+    def finish(self, w):
+        for i in range(4): self.sibc(w, i).wait_send()
+        self.ca(w).wait_send(); self.cb(w).wait_send()
+        for h in (0, 1): self.cx(w, h).wait_send(); self.cy(w, h).wait_send()
+        for j in range(1, self.nz): self.zc(w, j).wait_send()
+
+def rs_kernel(*refs):
+    c, *refs = refs
+    take = lambda n: [refs.pop(0) for _ in range(n)]
+    grads = take(5); outs = take(5)
+    sibs, ras, rbs, rxs, rys, zss, zrs = (take(5) for _ in range(7))
+    cs, csend, crecv, send, recv = refs
+    s = Scatter(grads, sibs, ras, rbs, rxs, rys, zss, zrs, outs, cs, csend, crecv, send, recv)
+    greet(s.partners())
+    s.start_c(c[0, 0])
+    for w in (1, 0, 2, 3, 4): s.s0(w)
+    s.cc().wait_recv()
+    q, o, f, p, v = range(5)
+    s.a(o); s.a(v); s.a(q); s.r(o); s.r(v); s.a(f); s.r(q); s.f(o); s.f(v); s.a(p); s.r(f); s.f(q); s.r(p); s.f(f)
+    s.zf(o); s.zf(v); s.zf(q); s.f(p); s.zf(f); s.zf(p)
+    s.cc().wait_send()
+    for w in range(5): s.finish(w)
+
+def scatter_all(c, gq, go, gf, gp, gv):
+    nz = lax.axis_size("fsdp")
+    grads = (gq, go, gf, gp, gv)
+    blocks = [(gq.shape[0]//8, gq.shape[1]), (go.shape[0]//8, go.shape[1]), (gf.shape[0], gf.shape[1]//8), (gp.shape[0]//8, gp.shape[1]), gv.shape[1:]]
+    dt = [bf16]*4 + [f32]
+    hb = [(r//2, c_) for r, c_ in blocks]
+    piece = [(r, c_//nz) for r, c_ in blocks[:2]] + [(blocks[2][0]//nz, blocks[2][1]), (blocks[3][0], blocks[3][1]//nz), blocks[4]]
+    zs = [(nz,)+piece[0], (nz,)+piece[1]] + blocks[2:]
+    zr = [(nz-1,)+s for s in piece]
+    V = lambda ss: [pltpu.VMEM(s, t) for s, t in zip(ss, dt)]
+    vm = pl.BlockSpec(memory_space=pltpu.VMEM)
+    return pl.pallas_call(rs_kernel, out_shape=[jax.ShapeDtypeStruct(s, f32) for s in piece],
+        in_specs=[pl.BlockSpec(memory_space=pltpu.SMEM)] + [vm]*5, out_specs=[vm]*5,
+        scratch_shapes=V([(4,)+b for b in blocks]) + V(hb) + V(hb) + V(blocks) + V(blocks) + V(zs) + V(zr)
+            + [pltpu.VMEM((2, 8, 128), f32), pltpu.SemaphoreType.DMA, pltpu.SemaphoreType.DMA, pltpu.SemaphoreType.DMA((5, 13)), pltpu.SemaphoreType.DMA((5, 13))],
+        compiler_params=pltpu.CompilerParams(collective_id=1, has_side_effects=True, vmem_limit_bytes=60<<20))(c, *grads)
+
 
 HD = 64
 
@@ -107,43 +357,25 @@
     head_count = width // head_size
     block_rows = min(512, seq_len)
     scaling = head_size ** (-0.5)
-    low_qkv = qkv_weight.astype(jnp.bfloat16)
-    low_out = out_weight.astype(jnp.bfloat16)
-    low_fc = fc_weight.astype(jnp.bfloat16)
-    low_proj = proj_weight.astype(jnp.bfloat16)
-    attn_cols = (
-        lax.all_gather(low_qkv, "dp", axis=1, tiled=True),
-        lax.all_gather(low_out, "dp", axis=1, tiled=True),
-        lax.all_gather(vectors.astype(jnp.bfloat16), "dp", axis=1, tiled=True),
-    )
-    weight_qkv, weight_out = (
-        lax.all_gather(attn_cols[0], "fsdp", axis=0, tiled=True),
-        lax.all_gather(attn_cols[1], "fsdp", axis=0, tiled=True),
-    )
-    vector_rows = attn_cols[2].astype(jnp.float32)
-    gain_one, shift_one, query_shift, value_shift = (
-        vector_rows[0],
-        vector_rows[1],
-        vector_rows[2],
-        vector_rows[3],
-    )
-    out_shift, gain_two, shift_two, proj_shift = (
-        vector_rows[4],
-        vector_rows[5],
-        vector_rows[6],
-        vector_rows[7],
-    )
+    ndp = lax.axis_size("dp")
+    rows = fc_bias.shape[0] // 128 + vectors.size // 128 if ndp == 8 else 0
+    if ndp == 8:
+        small = jnp.concatenate([fc_bias.reshape(-1, 128), vectors.reshape(-1, 128)], axis=0)
+        small = jnp.pad(small, ((0, 16 - small.shape[0]), (0, 0)))
+        QT, OT, weight_fc, PT, small = gather_all(
+            qkv_weight.astype(bf16).T, out_weight.astype(bf16).T, fc_weight.astype(bf16), proj_weight.astype(bf16).T, small)
+        nb = fc_bias.shape[0] // 128
+        fc_shift = small[:, :nb].reshape(-1).astype(bf16).astype(f32)
+        vector_rows = small[:, nb:rows].reshape(ndp, vectors.shape[0], vectors.shape[1]).transpose(1, 0, 2).reshape(vectors.shape[0], -1)
+        vector_rows = vector_rows.astype(bf16).astype(f32)
+        weight_qkv, weight_out, weight_proj = QT.T, OT.T, PT.T
+    else:
+        g = lambda a: lax.all_gather(lax.all_gather(a.astype(bf16), "dp", axis=1, tiled=True), "fsdp", axis=0, tiled=True)
+        weight_qkv, weight_out, weight_fc, weight_proj = g(qkv_weight), g(out_weight), g(fc_weight), g(proj_weight)
+        vector_rows = lax.all_gather(vectors.astype(bf16), "dp", axis=1, tiled=True).astype(f32)
+        fc_shift = lax.all_gather(fc_bias.astype(bf16), "dp", axis=0, tiled=True).astype(f32)
+    gain_one, shift_one, query_shift, value_shift, out_shift, gain_two, shift_two, proj_shift = vector_rows
     qkv_shift = jnp.concatenate([query_shift, jnp.zeros_like(query_shift), value_shift])
-    mlp_cols = (
-        lax.all_gather(low_fc, "dp", axis=1, tiled=True),
-        lax.all_gather(low_proj, "dp", axis=1, tiled=True),
-        lax.all_gather(fc_bias.astype(jnp.bfloat16), "dp", axis=0, tiled=True),
-    )
-    weight_fc, weight_proj = (
-        lax.all_gather(mlp_cols[0], "fsdp", axis=0, tiled=True),
-        lax.all_gather(mlp_cols[1], "fsdp", axis=0, tiled=True),
-    )
-    fc_shift = mlp_cols[2].astype(jnp.float32)
     seq = 0
     inputs = tokens.astype(jnp.float32)
     length = lengths[seq]
@@ -167,22 +399,7 @@
     saved = [
         (inputs, normed_one, heads_view, log_sums, attended, middle, normed_two, hidden, activated)
     ]
-    back_mlp = (
-        lax.all_gather(low_fc, "dp", axis=1, tiled=True),
-        lax.all_gather(low_proj, "dp", axis=1, tiled=True),
-    )
-    back_fc, back_proj = (
-        lax.all_gather(back_mlp[0], "fsdp", axis=0, tiled=True),
-        lax.all_gather(back_mlp[1], "fsdp", axis=0, tiled=True),
-    )
-    back_attn = (
-        lax.all_gather(low_qkv, "dp", axis=1, tiled=True),
-        lax.all_gather(low_out, "dp", axis=1, tiled=True),
-    )
-    back_qkv, back_out = (
-        lax.all_gather(back_attn[0], "fsdp", axis=0, tiled=True),
-        lax.all_gather(back_attn[1], "fsdp", axis=0, tiled=True),
-    )
+    back_fc, back_proj, back_qkv, back_out = weight_fc, weight_proj, weight_qkv, weight_out
     seq = 0
     inputs, normed_one, heads_view, log_sums, attended, middle, normed_two, hidden, activated = (
         saved[seq]
@@ -247,31 +464,16 @@
     grad_norm = jnp.sqrt(squares)
     factor = jnp.minimum(1.0, clip_norm / grad_norm)
     ratios = [grad_norm / clip_norm]
-    weighted = tuple((factor * member for member in per_seq))
-    column_sums = (
-        lax.psum_scatter(weighted[0], "dp", scatter_dimension=1, tiled=True),
-        lax.psum_scatter(weighted[1], "dp", scatter_dimension=1, tiled=True),
-        lax.psum_scatter(weighted[2], "dp", scatter_dimension=1, tiled=True),
-        lax.psum_scatter(weighted[3], "dp", scatter_dimension=1, tiled=True),
-        lax.psum_scatter(weighted[4], "dp", scatter_dimension=0, tiled=True),
-        lax.psum_scatter(weighted[5], "dp", scatter_dimension=1, tiled=True),
-    )
-    row_sums = (
-        lax.psum_scatter(
-            column_sums[0].astype(jnp.bfloat16), "fsdp", scatter_dimension=0, tiled=True
-        ).astype(jnp.float32),
-        lax.psum_scatter(
-            column_sums[1].astype(jnp.bfloat16), "fsdp", scatter_dimension=0, tiled=True
-        ).astype(jnp.float32),
-        lax.psum_scatter(
-            column_sums[2].astype(jnp.bfloat16), "fsdp", scatter_dimension=0, tiled=True
-        ).astype(jnp.float32),
-        lax.psum_scatter(
-            column_sums[3].astype(jnp.bfloat16), "fsdp", scatter_dimension=0, tiled=True
-        ).astype(jnp.float32),
-    )
-    small_sums = lax.psum((column_sums[4], column_sums[5]), "fsdp")
-    finals = (row_sums[0], row_sums[1], row_sums[2], row_sums[3], small_sums[0], small_sums[1])
+    if ndp == 8:
+        nb = fc_bias.shape[0] // 128
+        gv = jnp.concatenate([grad_fshift.reshape(ndp, nb, 128), grad_vec.reshape(8, ndp, -1).transpose(1, 0, 2).reshape(ndp, -1, 128)], axis=1)
+        gv = jnp.pad(gv, ((0, 0), (0, 16 - gv.shape[1]), (0, 0)))
+        sq, so, sf, sp, sv = scatter_all(factor.reshape(1, 1), grad_qkv.T.astype(bf16), grad_out.T.astype(bf16), grad_fc.astype(bf16), grad_proj.T.astype(bf16), gv)
+        finals = (sq.T, so.T, sf, sp.T, sv[:nb].reshape(-1), sv[nb:rows].reshape(vectors.shape))
+    else:
+        ps = lambda a, dim: lax.psum_scatter(factor * a, "dp", scatter_dimension=dim, tiled=True)
+        pz = lambda a: lax.psum_scatter(a.astype(bf16), "fsdp", scatter_dimension=0, tiled=True).astype(f32)
+        finals = tuple(pz(ps(a, 1)) for a in per_seq[:4]) + lax.psum((ps(per_seq[4], 0), ps(per_seq[5], 1)), "fsdp")
     examples = lax.axis_size("dp") * lax.axis_size("fsdp") * seq_count
     return (
         outputs,

time: 991 us -> 610 us (0.62)
  waiting for transfers between devices: 446 us -> 0 us
  Pallas kernels: 0 us -> 191 us
  blocking collectives: 76.6 us -> 0 us
  other arithmetic: 127 us -> 101 us
  between operations: 22.1 us -> 8.19 us
    pallas_call x0 -> x2, Pallas kernels: none -> 191 us  [the longest x1 99.4 us: scatter_all(): pl.pallas_call(rs_kernel, out_shape=[jax.ShapeDtypeStruct(s, f32) for s i...]
    all_gather x6 -> x0, waiting for transfers between devices: 159 us -> none  [the longest x1 71.8 us: shards(): lax.all_gather(attn_cols[0], 'fsdp', axis=0, tiled=True)]
    unnamed x19 -> x0, waiting for transfers between devices: 150 us -> none
    reduce_scatter x5 -> x0, waiting for transfers between devices: 137 us -> none  [the longest x1 64 us: shards(): lax.psum_scatter(weighted[2], 'dp', scatter_dimension=1, tiled=True)]
    all_gather x4 -> x0, blocking collectives: 41.7 us -> none  [the longest x1 14.5 us: shards(): lax.all_gather(low_qkv, 'dp', axis=1, tiled=True)]
    mul x6 -> x0, other arithmetic: 27.3 us -> none  [shards(): weighted = tuple((factor * member for member in per_seq))]
    unnamed x1 -> x0, blocking collectives: 23 us -> none
    unnamed x139 -> x125, local copies, waits for them, and re-layouts: 54.3 us -> 32.6 us
  transfers between devices with their start and end apart: 15 -> 0, of which waited for: 11 -> 0; matrix products, arithmetic and copies ran while one was open for 20% -> 0% of each run, Pallas kernels for 0% -> 0%
where the time goes in v1:
time: 610 us; the launch traced here: 600 us
  matrix products  233 us (38%)
  Pallas kernels  191 us (31%)
  other arithmetic  101 us (17%)
  local copies, waits for them, and re-layouts  66.9 us (11%)
  between operations  8.19 us (1%)
    pallas_call x1, Pallas kernels, scatter_all(): pl.pallas_call(rs_kernel, out_shape=[jax.ShapeDtypeStruct(s, f32) for s i...  99.4 us
    pallas_call x1, Pallas kernels, gather_all(): pl.pallas_call(ag_kernel, out_shape=[jax.ShapeDtypeStruct(s, bf16) for s...  91.6 us
    dot_general x2, matrix products, attend_back(): jnp.einsum('qhd,khd->hqk', grad_block, value_rows, preferred_element_type...  40.5 us
    convert_element_type x2, other arithmetic, attend_back(): grad_scores = (chances * (grad_chances - inner)).astype(jnp.bfloat16)  40.3 us
    unnamed x125, local copies, waits for them, and re-layouts  32.6 us
    dot_general x2, matrix products, masked_scores(): jnp.einsum('qhd,khd->hqk', query_rows, key_rows, preferred_element_type=j...  26.2 us
    dot_general x2, matrix products, attend_back(): jnp.einsum('hqk,qhd->khd', chances.astype(jnp.bfloat16), grad_block, pref...  24.7 us
    reduce_sum x2, other arithmetic, attend(): row_total = jnp.sum(powers, axis=-1, keepdims=True)  24.6 us

profile of v1, /device:TPU:0, one launch (start us, length us, event | category | flops | bytes accessed | tf_op | source)
XLA Modules:
  0.0 600.2 jit_solution(16814825723008090151)
XLA Ops:
  2.7 1.3 select_maximum_fusion.1.sv
  4.6 1.6 copy.49
  6.2 1.6 copy.62
  7.8 1.7 copy.48
  9.6 1.6 convert_element_type.152.sf
  11.2 1.6 convert_bitcast_fusion.3.sp
  12.8 1.8 copy.61
  14.7 1.3 fusion.34
  16.0 1.9 copy.47
  18.7 2.6 copy.52
  21.3 91.6 %shard_map.223 = (bf16[2304,768]{1,0:T(8,128)(2,1)}, bf16[768,768]{1,0:T(8,128)(2,1)}, bf16[768,3072]{1,0:T(8,128)(2,1)}, bf16[768,3072]{1,0:T(8,128)(2,1)}, f32[8,16,128]{2,1,0:T(8,128)}) custom-call(bf16[288,192]{1,0:T(8,128)(2,1)} %bitcast.138, bf16[96,192]{1,0:T(8,128)(2,1)} %bitcast.139, bf16[192,384]{1,0:T(8,128)(2,1)} %convert_element_type.152.sf, ...), custom_call_target="tpu_custom_call" | custom-call | tf_op jit(solution)/shard_map/pallas_call | solution.py:121
  115.7 8.1 %add_convert_fusion = bf16[1024,2304]{1,0:T(8,128)(2,1)} fusion(bf16[2304,768]{1,0:T(8,128)(2,1)} %get-tuple-element.20, f32[2304]{0:T(1024)S(1)} %pad_maximum_fusion.1, bf16[1024,768]{0,1:T(8,128)(2,1)S(1)} %copy.47, f32[768]{0:T(1024)S(1)} %add.174, f32[768]{0:T(1024)S(1)} %mul.232, f32[1024]{0:T(1024)S(1)} %fusion.52, f32[1024]{0:T(1024)S(1)} %broadcast_multiply_fusion.1), kind=kOutput, calls=%fused_computation.37 | convolution fusion | flops 3633315840 | bytes 9853952 | tf_op jit(solution)/shard_map/dot_general | solution.py:384
  123.8 6.7 %copy.50 = bf16[1024,2304]{0,1:T(8,128)(2,1)} copy(bf16[1024,2304]{1,0:T(8,128)(2,1)} %add_convert_fusion) | data formatting | bytes 9437184 | tf_op jit(solution)/shard_map/convert_element_type | solution.py:385
  130.5 14.4 %fusion.20 = (f32[12,512]{1,0:T(8,128)S(1)}, f32[12,512,1024]{2,1,0:T(8,128)}) fusion(pred[512,1024]{1,0:T(8,128)(4,1)S(1)} %get-tuple-element.73, bf16[1024,3,12,64]{0,3,2,1:T(8,128)(2,1)} %bitcast.111), kind=kOutput, calls=%fused_computation.39 | convolution fusion | flops 824174592 | bytes 28073984 | tf_op jit(solution)/shard_map/qhd,khd->hqk/dot_general | solution.py:274
  144.9 12.3 %fusion.1 = f32[12,512]{1,0:T(8,128)S(1)} fusion(f32[12,512]{1,0:T(8,128)S(1)} %get-tuple-element.74, f32[12,512,1024]{2,1,0:T(8,128)} %get-tuple-element.75, pred[512,1024]{1,0:T(8,128)(4,1)S(1)} %get-tuple-element.73), kind=kLoop, calls=%fused_computation.13 | loop fusion | flops 25159680 | bytes 25739264 | tf_op jit(solution)/shard_map/reduce_sum | solution.py:292
  157.8 2.5 copy-done
  160.3 9.0 %fusion.42 = bf16[512,12,64]{0,2,1:T(8,128)(2,1)} fusion(f32[12,512]{1,0:T(8,128)S(1)} %fusion.1, f32[12,512]{1,0:T(8,128)S(1)} %get-tuple-element.74, f32[12,512,1024]{2,1,0:T(8,128)S(1)} %copy-done, pred[512,1024]{1,0:T(8,128)(4,1)S(1)} %get-tuple-element.73, bf16[1024,3,12,64]{0,3,2,1:T(8,128)(2,1)S(1)} %bitcast.114), kind=kOutput, calls=%fused_computation.89 | convolution fusion | flops 837156864 | bytes 28114944 | tf_op jit(solution)/shard_map/hqk,khd->qhd/dot_general | solution.py:295
  169.3 11.8 %fusion.19 = (f32[12,512]{1,0:T(8,128)S(1)}, f32[12,512,1024]{2,1,0:T(8,128)}) fusion(pred[512,1024]{1,0:T(8,128)(4,1)} %get-tuple-element.72, bf16[1024,3,12,64]{0,3,2,1:T(8,128)(2,1)S(1)} %bitcast.115), kind=kOutput, calls=%fused_computation.38 | convolution fusion | flops 824174592 | bytes 28073984 | tf_op jit(solution)/shard_map/qhd,khd->hqk/dot_general | solution.py:274
  181.1 12.3 %fusion = f32[12,512]{1,0:T(8,128)S(1)} fusion(f32[12,512]{1,0:T(8,128)S(1)} %get-tuple-element.76, f32[12,512,1024]{2,1,0:T(8,128)} %get-tuple-element.77, pred[512,1024]{1,0:T(8,128)(4,1)S(1)} %copy-done.14), kind=kLoop, calls=%fused_computation.12 | loop fusion | flops 25159680 | bytes 25739264 | tf_op jit(solution)/shard_map/reduce_sum | solution.py:292
  194.1 2.4 copy-done.1
  196.5 9.2 %fusion.41 = bf16[512,12,64]{0,2,1:T(8,128)(2,1)} fusion(f32[12,512]{1,0:T(8,128)S(1)} %fusion, f32[12,512]{1,0:T(8,128)S(1)} %get-tuple-element.76, f32[12,512,1024]{2,1,0:T(8,128)S(1)} %copy-done.1, pred[512,1024]{1,0:T(8,128)(4,1)S(1)} %copy-done.14, bf16[1024,3,12,64]{0,3,2,1:T(8,128)(2,1)S(1)} %bitcast.116), kind=kOutput, calls=%fused_computation.88 | convolution fusion | flops 837156864 | bytes 28114944 | tf_op jit(solution)/shard_map/hqk,khd->qhd/dot_general | solution.py:295
  205.8 1.5 pad_maximum_fusion
  207.3 3.8 fusion.73
  211.6 5.5 fusion.67
  217.2 4.5 copy-done.16
  221.7 6.5 %add_convert_fusion.2 = bf16[1024,768]{0,1:T(8,128)(2,1)} fusion(f32[1024,768]{0,1:T(8,128)S(1)} %get-tuple-element.79, bf16[768,3072]{1,0:T(8,128)(2,1)S(1)} %bitcast.144, f32[768]{0:T(1024)S(1)} %copy-done.43, f32[1024,3072]{1,0:T(8,128)S(1)} %fusion.67, f32[3072]{0:T(1024)S(1)} %copy-done.38), kind=kOutput, calls=%fused_computation.71 | convolution fusion | flops 4865654784 | bytes 22035456 | tf_op jit(solution)/shard_map/dot_general | solution.py:396
  228.1 2.6 copy.63
  230.7 21.7 %convert_reduce_fusion = (f32[3072]{0:T(1024)S(1)}, bf16[1024,3072]{1,0:T(8,128)(2,1)}) fusion(f32[1024,3072]{1,0:T(8,128)} %copy-done.16, f32[3072]{0:T(1024)S(1)} %copy-done.38, bf16[768,3072]{1,0:T(8,128)(2,1)} %get-tuple-element.23, bf16[1024,768]{0,1:T(8,128)(2,1)} %copy.52, f32[1024]{0:T(1024)S(1)} %copy-done.32), kind=kOutput, calls=%fused_computation.27 | convolution fusion | flops 4906546176 | bytes 25194496 | tf_op jit(solution)/shard_map/dot_general | solution.py:413
  252.4 11.0 %multiply_reduce_fusion.2 = (f32[]{:T(128)}, bf16[3072,768]{1,0:T(8,128)(2,1)}) fusion(bf16[1024,768]{0,1:T(8,128)(2,1)S(1)} %copy-done.10, f32[1024]{0:T(1024)S(1)} %copy-done.32, f32[1024,3072]{1,0:T(8,128)S(1)} %copy-done.17, f32[3072]{0:T(1024)S(1)} %copy-done.38), kind=kOutput, calls=%fused_computation.35 | convolution fusion | flops 4872732672 | bytes 18890756 | tf_op jit(solution)/shard_map/dot_general | solution.py:411
  263.4 9.7 %fusion.75 = (f32[768]{0:T(1024)S(1)}, f32[1024,768]{1,0:T(8,128)}) fusion(bf16[1024,3072]{1,0:T(8,128)(2,1)} %get-tuple-element.91, bf16[768,3072]{1,0:T(8,128)(2,1)} %get-tuple-element.22), kind=kOutput, calls=%fused_computation.166 | convolution fusion | flops 4832623616 | bytes 14158848 | tf_op jit(solution)/shard_map/dot_general | solution.py:418
  273.8 3.7 copy.53
  277.4 6.7 %copy.59 = bf16[3072,768]{0,1:T(8,128)(2,1)} copy(bf16[3072,768]{1,0:T(8,128)(2,1)} %get-tuple-element.89) | data formatting | bytes 9437184 | tf_op jit(solution)/shard_map/dot_general | solution.py:411
  286.0 2.8 multiply_reduce_fusion.5
  288.8 10.8 %fusion.70 = (bf16[768,3072]{1,0:T(8,128)(2,1)}, f32[]{:T(128)}) fusion(bf16[1024,3072]{1,0:T(8,128)(2,1)} %get-tuple-element.91, f32[1024,768]{0,1:T(8,128)S(1)} %get-tuple-element.79, f32[768]{0:T(1024)S(1)} %add.185, f32[768]{0:T(1024)S(1)} %mul.240, f32[1024]{0:T(1024)S(1)} %fusion.53, f32[1024]{0:T(1024)S(1)} %broadcast_multiply_fusion), kind=kOutput, calls=%fused_computation.161 | convolution fusion | flops 4842848256 | bytes 14170116 | tf_op jit(solution)/shard_map/dot_general | solution.py:416
  299.6 2.5 fusion.69
  302.2 3.3 convert_reduce_fusion.4
  305.5 3.0 multiply_reduce_fusion.8
  308.5 2.4 copy.58
  311.0 2.8 convolution_convert_fusion
  314.0 11.4 %fusion.11 = f32[12,64,1024]{2,1,0:T(8,128)S(1)} fusion(bf16[512,12,64]{0,2,1:T(8,128)(2,1)S(1)} %bitcast.132, f32[12,512]{1,0:T(8,128)S(1)} %copy-done.23, f32[12,512,1024]{2,1,0:T(8,128)} %get-tuple-element.75, pred[512,1024]{1,0:T(8,128)(4,1)S(1)} %copy-done.13), kind=kOutput, calls=%fused_computation.25 | convolution fusion | flops 830472192 | bytes 29646848 | tf_op jit(solution)/shard_map/hqk,qhd->khd/dot_general | solution.py:310
  325.4 13.3 %add_bitcast_fusion = bf16[1024,1,12,64]{0,3,2,1:T(8,128)(2,1)} fusion(f32[12,64,1024]{2,1,0:T(8,128)S(1)} %fusion.11, bf16[512,12,64]{0,2,1:T(8,128)(2,1)S(1)} %bitcast.134, f32[12,512]{1,0:T(8,128)S(1)} %copy-done.24, f32[12,512,1024]{2,1,0:T(8,128)} %get-tuple-element.77, pred[512,1024]{1,0:T(8,128)(4,1)S(1)} %copy-done.15), kind=kOutput, calls=%fused_computation.65 | convolution fusion | flops 832045056 | bytes 31219712 | tf_op jit(solution)/shard_map/hqk,qhd->khd/dot_general | solution.py:310
  338.7 20.2 %multiply_reduce_fusion.1 = (f32[12,512]{1,0:T(8,128)S(1)}, f32[12,512,1024]{2,1,0:T(8,128)}) fusion(f32[12,512]{1,0:T(8,128)S(1)} %copy-done.24, f32[12,512,1024]{2,1,0:T(8,128)} %get-tuple-element.77, pred[512,1024]{1,0:T(8,128)(4,1)S(1)} %copy-done.15, bf16[512,12,64]{0,2,1:T(8,128)(2,1)S(1)} %bitcast.135, bf16[1024,3,12,64]{0,3,2,1:T(8,128)(2,1)} %bitcast.112), kind=kOutput, calls=%fused_computation.4 | convolution fusion | flops 836757504 | bytes 53264384 | tf_op jit(solution)/shard_map/qhd,khd->hqk/dot_general | solution.py:316
  358.9 21.4 %multiply_convert_fusion.1 = bf16[12,512,1024]{2,1,0:T(8,128)(2,1)} fusion(f32[12,512,1024]{2,1,0:T(8,128)} %get-tuple-element.81, f32[12,512]{1,0:T(8,128)S(1)} %get-tuple-element.80, f32[12,512]{1,0:T(8,128)S(1)} %copy-done.24, f32[12,512,1024]{2,1,0:T(8,128)} %get-tuple-element.77, pred[512,1024]{1,0:T(8,128)(4,1)S(1)} %copy-done.15), kind=kLoop, calls=%fused_computation.3 | loop fusion | flops 37748736 | bytes 63488000 | tf_op jit(solution)/shard_map/convert_element_type | solution.py:320
  380.3 8.5 %multiply_bitcast_fusion.2 = bf16[512,12,64]{0,2,1:T(8,128)(2,1)S(1)} fusion(bf16[12,512,1024]{2,1,0:T(8,128)(2,1)} %multiply_convert_fusion.1, bf16[1024,3,12,64]{0,3,2,1:T(8,128)(2,1)S(1)} %bitcast.119), kind=kOutput, calls=%fused_computation.85 | convolution fusion | flops 806092800 | bytes 14942208 | tf_op jit(solution)/shard_map/hqk,khd->qhd/dot_general | solution.py:322
  388.8 8.5 %fusion.50 = f32[12,64,1024]{2,1,0:T(8,128)} fusion(bf16[12,512,1024]{2,1,0:T(8,128)(2,1)} %multiply_convert_fusion.1, bf16[1024,3,12,64]{0,3,2,1:T(8,128)(2,1)S(1)} %bitcast.120), kind=kOutput, calls=%fused_computation.98 | convolution fusion | flops 805306368 | bytes 16515072 | tf_op jit(solution)/shard_map/hqk,qhd->khd/dot_general | solution.py:327
  397.3 20.3 %multiply_reduce_fusion = (f32[12,512]{1,0:T(8,128)S(1)}, f32[12,512,1024]{2,1,0:T(8,128)}) fusion(f32[12,512]{1,0:T(8,128)S(1)} %copy-done.23, f32[12,512,1024]{2,1,0:T(8,128)} %get-tuple-element.75, pred[512,1024]{1,0:T(8,128)(4,1)S(1)} %copy-done.13, bf16[512,12,64]{0,2,1:T(8,128)(2,1)S(1)} %bitcast.133, bf16[1024,3,12,64]{0,3,2,1:T(8,128)(2,1)} %bitcast.113), kind=kOutput, calls=%fused_computation.1 | convolution fusion | flops 836757504 | bytes 53264384 | tf_op jit(solution)/shard_map/qhd,khd->hqk/dot_general | solution.py:316
  417.6 18.9 %multiply_convert_fusion = bf16[12,512,1024]{2,1,0:T(8,128)(2,1)S(1)} fusion(f32[12,512,1024]{2,1,0:T(8,128)} %get-tuple-element.83, f32[12,512]{1,0:T(8,128)S(1)} %get-tuple-element.82, f32[12,512]{1,0:T(8,128)S(1)} %copy-done.23, f32[12,512,1024]{2,1,0:T(8,128)} %get-tuple-element.75, pred[512,1024]{1,0:T(8,128)(4,1)S(1)} %copy-done.13), kind=kLoop, calls=%fused_computation | loop fusion | flops 37748736 | bytes 63488000 | tf_op jit(solution)/shard_map/convert_element_type | solution.py:320
  436.5 4.6 copy-done.2
  441.1 2.4 multiply_bitcast_fusion
  443.5 8.6 %multiply_bitcast_fusion.1 = bf16[512,12,64]{0,2,1:T(8,128)(2,1)S(1)} fusion(bf16[12,512,1024]{2,1,0:T(8,128)(2,1)} %copy-done.2, bf16[1024,3,12,64]{0,3,2,1:T(8,128)(2,1)S(1)} %bitcast.124), kind=kOutput, calls=%fused_computation.84 | convolution fusion | flops 806092800 | bytes 14942208 | tf_op jit(solution)/shard_map/hqk,khd->qhd/dot_general | solution.py:322
  452.3 1.0 convert_reduce_fusion.1
  454.4 5.8 fusion.74
  460.2 6.5 %multiply_reduce_fusion.4 = (f32[]{:T(128)}, bf16[768,2304]{1,0:T(8,128)(2,1)}) fusion(bf16[1024,2304]{0,1:T(8,128)(2,1)S(1)} %bitcast.130, bf16[1024,768]{0,1:T(8,128)(2,1)S(1)} %copy-done.5, f32[768]{0:T(1024)S(1)} %copy-done.42, f32[768]{0:T(1024)S(1)} %copy-done.31, f32[1024]{0:T(1024)S(1)} %copy-done.34, f32[1024]{0:T(1024)S(1)} %copy-done.28), kind=kOutput, calls=%fused_computation.40 | convolution fusion | flops 3633905664 | bytes 9844740 | tf_op jit(solution)/shard_map/dot_general | solution.py:444
  469.9 3.5 copy.54
  473.4 5.7 copy.57
  479.5 2.6 fusion.31
  482.4 1.3 fusion.29
  483.8 1.7 add_convert_fusion.1
  485.5 1.8 copy.64
  489.7 99.4 %shard_map.224 = (f32[288,192]{1,0:T(8,128)}, f32[96,192]{1,0:T(8,128)}, f32[192,384]{1,0:T(8,128)}, f32[96,768]{1,0:T(8,128)}, f32[16,128]{1,0:T(8,128)}) custom-call(f32[1,1]{1,0:T(1,128)} %bitcast.25.refs_0_, bf16[2304,768]{1,0:T(8,128)(2,1)} %bitcast.126, bf16[768,768]{1,0:T(8,128)(2,1)} %bitcast.131, bf16[768,3072]{1,0:T(8,128)(2,1)} %get-tuple-element.65.refs_3_, ...), custom_call_target="tpu_custom_call" | custom-call | tf_op jit(solution)/shard_map/pallas_call | solution.py:249
  589.1 1.0 bitcast_add_fusion.1
  592.6 1.3 bitcast_add_fusion.3
  595.2 1.7 multiply_add_fusion
  596.9 1.7 bitcast_add_fusion
  (180 shorter events, 16.8 us)
Async XLA Ops:
  16.0 141.8 %copy-start.12 = (pred[512,1024]{1,0:T(8,128)(4,1)}, pred[512,1024]{1,0:T(8,128)(4,1)S(1)}, u32[]{:S(2)}) copy-start(pred[512,1024]{1,0:T(8,128)(4,1)S(1)} %get-tuple-element.73) | copy-start | bytes 1572868
  17.9 105.9 %copy-start.4 = (bf16[1024,768]{0,1:T(8,128)(2,1)}, bf16[1024,768]{0,1:T(8,128)(2,1)S(1)}, u32[]{:S(2)}) copy-start(bf16[1024,768]{0,1:T(8,128)(2,1)S(1)} %copy.47) | copy-start | bytes 4718596
  18.2 105.6 %copy-start.27 = (f32[1024]{0:T(1024)}, f32[1024]{0:T(1024)S(1)}, u32[]{:S(2)}) copy-start(f32[1024]{0:T(1024)S(1)} %broadcast_multiply_fusion.1) | copy-start | bytes 12292
  18.7 94.2 %copy-start.35 = (f32[1024]{0:T(1024)}, f32[1024]{0:T(1024)S(1)}, u32[]{:S(2)}) copy-start(f32[1024]{0:T(1024)S(1)} %fusion.30) | copy-start | bytes 12292
  18.7 105.1 %copy-start.33 = (f32[1024]{0:T(1024)}, f32[1024]{0:T(1024)S(1)}, u32[]{:S(2)}) copy-start(f32[1024]{0:T(1024)S(1)} %fusion.52) | copy-start | bytes 12292
  114.7 9.1 %copy-start.30 = (f32[768]{0:T(1024)}, f32[768]{0:T(1024)S(1)}, u32[]{:S(2)}) copy-start(f32[768]{0:T(1024)S(1)} %mul.232) | copy-start | bytes 9220
  114.8 9.0 %copy-start.41 = (f32[768]{0:T(1024)}, f32[768]{0:T(1024)S(1)}, u32[]{:S(2)}) copy-start(f32[768]{0:T(1024)S(1)} %add.174) | copy-start | bytes 9220
  130.5 27.3 %copy-start.3 = (bf16[1024,2304]{0,1:T(8,128)(2,1)S(1)}, bf16[1024,2304]{0,1:T(8,128)(2,1)}, u32[]{:S(2)}) copy-start(bf16[1024,2304]{0,1:T(8,128)(2,1)} %copy.50) | copy-start | bytes 14155780
  144.9 15.4 %copy-start = (f32[12,512,1024]{2,1,0:T(8,128)S(1)}, f32[12,512,1024]{2,1,0:T(8,128)}, u32[]{:S(2)}) copy-start(f32[12,512,1024]{2,1,0:T(8,128)} %get-tuple-element.75) | copy-start | bytes 75497472
  169.3 11.8 %copy-start.14 = (pred[512,1024]{1,0:T(8,128)(4,1)S(1)}, pred[512,1024]{1,0:T(8,128)(4,1)}, u32[]{:S(2)}) copy-start(pred[512,1024]{1,0:T(8,128)(4,1)} %get-tuple-element.72) | copy-start | bytes 1572868
  181.1 15.4 %copy-start.1 = (f32[12,512,1024]{2,1,0:T(8,128)S(1)}, f32[12,512,1024]{2,1,0:T(8,128)}, u32[]{:S(2)}) copy-start(f32[12,512,1024]{2,1,0:T(8,128)} %get-tuple-element.77) | copy-start | bytes 75497472
  207.3 3.9 copy-start.18
  207.3 4.3 slice-start.4
  207.3 4.3 slice-start.5
  207.3 14.3 %slice-start.6 = ((s8[4718592]{0:T(1024)(128)(4,1)}), s8[4194304]{0:T(1024)(128)(4,1)S(1)}, s32[]{:S(2)}) async-start(s8[4718592]{0:T(1024)(128)(4,1)} %bitcast.143), calls=%async_computation.6 | async-start | bytes 8388608
  211.6 10.1 %copy-start.38 = (f32[3072]{0:T(1024)S(1)}, f32[3072]{0:T(1024)}, u32[]{:S(2)}) copy-start(f32[3072]{0:T(1024)} %reshape.282) | copy-start | bytes 36868
  211.6 10.0 %copy-start.43 = (f32[768]{0:T(1024)S(1)}, f32[768]{0:T(1024)}, u32[]{:S(2)}) copy-start(f32[768]{0:T(1024)} %add.193) | copy-start | bytes 9220
  211.6 10.0 %slice-start.7 = ((s8[4718592]{0:T(1024)(128)(4,1)}), s8[524288]{0:T(1024)(128)(4,1)S(1)}, s32[]{:S(2)}) async-start(s8[4718592]{0:T(1024)(128)(4,1)} %bitcast.143), calls=%async_computation.7 | async-start | bytes 1048576
  217.2 4.5 copy-start.16
  221.7 9.1 %copy-start.32 = (f32[1024]{0:T(1024)S(1)}, f32[1024]{0:T(1024)}, u32[]{:S(2)}) copy-start(f32[1024]{0:T(1024)} %get-tuple-element.97) | copy-start | bytes 12292
  230.7 21.7 %copy-start.10 = (bf16[1024,768]{0,1:T(8,128)(2,1)S(1)}, bf16[1024,768]{0,1:T(8,128)(2,1)}, u32[]{:S(2)}) copy-start(bf16[1024,768]{0,1:T(8,128)(2,1)} %copy.52) | copy-start | bytes 4718596
  230.7 21.7 %copy-start.17 = (f32[1024,3072]{1,0:T(8,128)S(1)}, f32[1024,3072]{1,0:T(8,128)}, u32[]{:S(2)}) copy-start(f32[1024,3072]{1,0:T(8,128)} %copy-done.16) | copy-start | bytes 37748740
  288.8 10.8 %copy-start.8 = (f32[1024,768]{0,1:T(8,128)S(1)}, f32[1024,768]{0,1:T(8,128)}, u32[]{:S(2)}) copy-start(f32[1024,768]{0,1:T(8,128)} %copy.53) | copy-start | bytes 9437188
  302.1 3.3 copy-start.19
  311.0 2.9 copy-start.13
  311.0 2.9 copy-start.23
  314.0 11.4 %copy-start.15 = (pred[512,1024]{1,0:T(8,128)(4,1)S(1)}, pred[512,1024]{1,0:T(8,128)(4,1)}, u32[]{:S(2)}) copy-start(pred[512,1024]{1,0:T(8,128)(4,1)} %get-tuple-element.72) | copy-start | bytes 1572868
  314.0 11.4 %copy-start.24 = (f32[12,512]{1,0:T(8,128)S(1)}, f32[12,512]{1,0:T(8,128)}, u32[]{:S(2)}) copy-start(f32[12,512]{1,0:T(8,128)} %log_add_fusion.1) | copy-start | bytes 73732
  338.7 41.6 %slice-start = ((s8[4718592]{0:T(1024)(128)(4,1)}), s8[524288]{0:T(1024)(128)(4,1)S(1)}, s32[]{:S(2)}) async-start(s8[4718592]{0:T(1024)(128)(4,1)} %bitcast.117), calls=%async_computation | async-start | bytes 1048576
  358.9 21.4 %slice-start.1 = ((s8[4718592]{0:T(1024)(128)(4,1)}), s8[4194304]{0:T(1024)(128)(4,1)S(1)}, s32[]{:S(2)}) async-start(s8[4718592]{0:T(1024)(128)(4,1)} %bitcast.117), calls=%async_computation.1 | async-start | bytes 8388608
  397.3 43.8 %slice-start.2 = ((s8[4718592]{0:T(1024)(128)(4,1)}), s8[524288]{0:T(1024)(128)(4,1)S(1)}, s32[]{:S(2)}) async-start(s8[4718592]{0:T(1024)(128)(4,1)} %bitcast.121), calls=%async_computation.2 | async-start | bytes 1048576
  417.6 23.5 %slice-start.3 = ((s8[4718592]{0:T(1024)(128)(4,1)}), s8[4194304]{0:T(1024)(128)(4,1)S(1)}, s32[]{:S(2)}) async-start(s8[4718592]{0:T(1024)(128)(4,1)} %bitcast.121), calls=%async_computation.3 | async-start | bytes 8388608
  417.6 23.5 %copy-start.9 = (f32[12,64,1024]{2,1,0:T(8,128)S(1)}, f32[12,64,1024]{2,1,0:T(8,128)}, u32[]{:S(2)}) copy-start(f32[12,64,1024]{2,1,0:T(8,128)} %fusion.50) | copy-start | bytes 9437188
  436.5 4.6 copy-start.2
  443.5 8.8 %copy-start.20 = (bf16[1024,1,12,64]{0,3,2,1:T(8,128)(2,1)S(1)}, bf16[1024,1,12,64]{0,3,2,1:T(8,128)(2,1)}, u32[]{:S(2)}) copy-start(bf16[1024,1,12,64]{0,3,2,1:T(8,128)(2,1)} %add_bitcast_fusion) | copy-start | bytes 4718596
  452.3 2.0 copy-start.45
  454.3 5.8 copy-start.5
  454.3 5.8 copy-start.28
  454.3 5.8 copy-start.31
  454.3 5.8 copy-start.34
  454.3 5.8 copy-start.42
  473.4 8.7 %copy-start.36 = (f32[1024]{0:T(1024)S(1)}, f32[1024]{0:T(1024)}, u32[]{:S(2)}) copy-start(f32[1024]{0:T(1024)} %copy-done.35) | copy-start | bytes 12292
  479.5 2.8 copy-start.6
  479.5 4.2 copy-start.7
  479.5 4.2 copy-start.11
  483.7 3.6 copy-start.39
  483.7 5.1 copy-start.37
  483.8 5.2 copy-start.29
  489.7 99.4 %copy-start.21 = (f32[192,288]{0,1:T(8,128)S(1)}, f32[192,288]{0,1:T(8,128)}, u32[]{:S(2)}) copy-start(f32[192,288]{0,1:T(8,128)} %copy.61) | copy-start | bytes 663556
  489.7 101.3 %copy-start.22 = (f32[192,96]{0,1:T(8,128)S(1)}, f32[192,96]{0,1:T(8,128)}, u32[]{:S(2)}) copy-start(f32[192,96]{0,1:T(8,128)} %copy.62) | copy-start | bytes 221188
  489.7 102.9 %copy-start.44 = (f32[384]{0:T(512)S(1)}, f32[384]{0:T(512)}, u32[]{:S(2)}) copy-start(f32[384]{0:T(512)} %param.30) | copy-start | bytes 4612
  489.7 105.0 %copy-start.40 = (f32[8,96]{1,0:T(8,128)S(1)}, f32[8,96]{1,0:T(8,128)}, u32[]{:S(2)}) copy-start(f32[8,96]{1,0:T(8,128)} %param.31) | copy-start | bytes 9220
  489.7 105.6 %copy-start.25 = (f32[192,384]{1,0:T(8,128)S(1)}, f32[192,384]{1,0:T(8,128)}, u32[]{:S(2)}) copy-start(f32[192,384]{1,0:T(8,128)} %param.28) | copy-start | bytes 884740
  489.7 107.3 %copy-start.26 = (f32[768,96]{0,1:T(8,128)S(1)}, f32[768,96]{0,1:T(8,128)}, u32[]{:S(2)}) copy-start(f32[768,96]{0,1:T(8,128)} %param.29) | copy-start | bytes 884740

commit v2 on v0

v2 whole, which is shorter than its diff:
```python
import functools
import jax
import jax.numpy as jnp
from jax import lax
from jax.experimental import pallas as pl
from jax.experimental.pallas import tpu as pltpu
from jax.sharding import PartitionSpec as P

MESH = pl.DeviceIdType.MESH
f32 = jnp.float32
bf16 = jnp.bfloat16
HD=64; T=256; QB=256
EPS=1e-05
GC=0.7978845608028654
GA=0.044715

def nn(a, b): return lax.dot_general(a, b, (((1,), (0,)), ((), ())), preferred_element_type=f32)
def nt(a, b): return lax.dot_general(a, b, (((1,), (1,)), ((), ())), preferred_element_type=f32)
def at(i, n): return pl.ds(pl.multiple_of(i * n, n), n)
def loop(n, body): lax.fori_loop(0, n, lambda i, c: (body(i), c)[1], 0)

class Block:
    def __init__(s, **refs): s.__dict__.update(refs)
    def unpack(s):
        V = s.V
        n = V.shape[0]; w = s.x.shape[1] // n; k = s.bf.shape[1] // n // 128
        s.vec[...] = jnp.concatenate([V[d][0:8, 0:w] for d in range(n)], axis=1).astype(bf16).astype(f32)
        s.bf[...] = jnp.concatenate([V[d][8 + j:9 + j, :] for d in range(n) for j in range(k)], axis=1).astype(bf16).astype(f32)
        s.clear()
    def clear(s):
        s.col[...] = jnp.zeros_like(s.col); s.ssq[...] = jnp.zeros_like(s.ssq)
        L = s.x.shape[0]
        kp = lax.broadcasted_iota(jnp.int32, (L, 128), 0)
        s.kb[...] = jnp.where(kp < s.length, 0.0, -1e30).astype(bf16)
    def row(s, i): return s.vec[i:i + 1, :]
    def ln1(s):
        def body(i):
            x = s.x[at(i, T), :].astype(f32)
            c = x - jnp.mean(x, axis=1, keepdims=True)
            v = jnp.mean(c * c, axis=1, keepdims=True)
            s.n1[at(i, T), :] = (c * lax.rsqrt(v + EPS) * s.row(0) + s.row(1)).astype(bf16)
        loop(s.x.shape[0] // T, body)
    def qkv(s):
        D = s.x.shape[1]
        for part, b in ((0, 2), (1, None), (2, 3)):
            def body(i):
                o = nt(s.n1[...], s.QT[pl.ds(pl.multiple_of(part * D + i * T, T), T), :])
                if b is not None: o = o + s.vec[b:b + 1, at(i, T)]
                s.m[:, pl.ds(pl.multiple_of(part * D + i * T, T), T)] = o.astype(bf16)
            loop(D // T, body)
    def heads(s, hp):
        D = s.x.shape[1]
        q = s.m[:, at(hp, 128)] * bf16(HD ** -0.5)
        k = s.m[:, pl.ds(pl.multiple_of(D + hp * 128, 128), 128)]
        v = s.m[:, pl.ds(pl.multiple_of(2 * D + hp * 128, 128), 128)]
        return q, k, v
    def masked(s, q, k, h):
        lane = lax.broadcasted_iota(jnp.int32, q.shape, 1)
        mine = (lane // HD) == h
        free = lane == (1 - h) * HD
        zero = jnp.zeros_like(q)
        return jnp.where(mine, q, jnp.where(free, jnp.ones_like(q), zero)), jnp.where(mine, k, jnp.where(free, s.kb[...], zero))
    def scores(s, kh, qh, b):
        qq = qh[b * QB:(b + 1) * QB]
        parts = []
        if b: parts.append(nt(kh[:b * QB], qq))
        o = nt(kh[b * QB:(b + 1) * QB], qq)
        r = lax.broadcasted_iota(jnp.int32, o.shape, 0); c = lax.broadcasted_iota(jnp.int32, o.shape, 1)
        parts.append(jnp.where(r <= c, o, -1e30))
        return parts
    def attend(s, hp):
        L = s.x.shape[0]
        q, k, v = s.heads(hp)
        vt = v.T
        outs = []
        for h in (0, 1):
            qh, kh = s.masked(q, k, h)
            for b in range(L // QB):
                parts = s.scores(kh, qh, b)
                mx = jnp.max(parts[-1], axis=0, keepdims=True)
                if b: mx = jnp.maximum(mx, jnp.max(parts[0], axis=0, keepdims=True))
                es = [jnp.exp(p - mx) for p in parts]
                l = sum(jnp.sum(e, axis=0, keepdims=True) for e in es)
                o = nn(vt[h * HD:(h + 1) * HD, b * QB:(b + 1) * QB], es[-1].astype(bf16))
                if b: o = o + nn(vt[h * HD:(h + 1) * HD, :b * QB], es[0].astype(bf16))
                s.lse[hp, h:h + 1, b * QB:(b + 1) * QB] = mx + jnp.log(l)
                s.ot[h * HD:(h + 1) * HD, b * QB:(b + 1) * QB] = o / l
        s.A[:, at(hp, 128)] = s.ot[...].T.astype(bf16)
    def out(s):
        def body(i):
            o = nt(s.A[...], s.OT[at(i, T), :])
            s.r[:, at(i, T)] = s.x[:, at(i, T)].astype(f32) + o + s.vec[4:5, at(i, T)]
        loop(s.x.shape[1] // T, body)
    def ln2(s):
        def body(i):
            x = s.r[at(i, T), :]
            c = x - jnp.mean(x, axis=1, keepdims=True)
            v = jnp.mean(c * c, axis=1, keepdims=True)
            s.n2[at(i, T), :] = (c * lax.rsqrt(v + EPS) * s.row(5) + s.row(6)).astype(bf16)
        loop(s.x.shape[0] // T, body)
    def fc(s):
        def body(i):
            f = nn(s.n2[...], s.F[:, at(i, T)]) + s.bf[:, at(i, T)]
            f2 = f * f
            t = jnp.tanh(f * (GC + GC * GA * f2))
            p = 0.5 * t + 0.5
            u = f * p
            s.u[:, at(i, T)] = u.astype(bf16)
            s.gp[:, at(i, T)] = (p + u * (1.0 - p) * (2 * GC + 6 * GC * GA * f2)).astype(bf16)
        loop(s.u.shape[1] // T, body)
    def ey_mask(s):
        def body(i):
            rp = i * T + lax.broadcasted_iota(jnp.int32, (T, s.x.shape[1]), 0)
            e = jnp.where(rp < s.length, s.ey[at(i, T), :].astype(f32), 0.0)
            s.ey[at(i, T), :] = e.astype(bf16)
            s.col[7:8, :] += jnp.sum(e, axis=0, keepdims=True)
        loop(s.x.shape[0] // T, body)
    def wgrad(s, lhs, rhs, out, nw, cols, first=0):
        N = cols; M = out.shape[0]
        def cp(i): return pltpu.make_async_copy(s.stage.at[i % 2, :, pl.ds(0, N)], out.at[at(i, T), :], s.dsem.at[i % 2])
        def body(i):
            s.lt[...] = lhs[:, at(i, T)].T
            @pl.when(i >= 2)
            def _(): cp(i - 2).wait()
            def inner(j):
                o = nn(s.lt[...], rhs[:, at(j, nw)])
                s.ssq[:, 0:nw] += jnp.sum(o * o, axis=0, keepdims=True)
                s.stage[i % 2, :, at(j, nw)] = o.astype(bf16)
            loop(N // nw, inner)
            cp(i).start()
        n = M // T
        loop(n, body)
        cp(n - 2).wait(); cp(n - 1).wait()
    def y(s):
        def body(i):
            o = nt(s.u[...], s.PT[at(i, T), :])
            s.er[:, at(i, T)] = (s.r[:, at(i, T)] + o + s.vec[7:8, at(i, T)]).astype(bf16)
        loop(s.x.shape[1] // T, body)
    def ef(s):
        def body(i):
            g = nn(s.ey[...], s.PT[:, at(i, T)]) * s.gp[:, at(i, T)].astype(f32)
            e = g.astype(bf16)
            s.gp[:, at(i, T)] = e
            s.dbf[:, at(i, T)] = jnp.sum(e.astype(f32), axis=0, keepdims=True)
        loop(s.u.shape[1] // T, body)
    def gn2(s):
        def body(i):
            s.G[:, at(i, T)] = nt(s.gp[...], s.F[at(i, T), :])
        loop(s.x.shape[1] // T, body)
    def lnb(s, x, gn, gain):
        c = x - jnp.mean(x, axis=1, keepdims=True)
        v = jnp.mean(c * c, axis=1, keepdims=True)
        rs = lax.rsqrt(v + EPS)
        h = c * rs
        a = gn * gain
        return h, rs * (a - jnp.mean(a, axis=1, keepdims=True) - h * jnp.mean(a * h, axis=1, keepdims=True))
    def ln2b(s):
        def body(i):
            gn = s.G[at(i, T), :]
            h, g = s.lnb(s.r[at(i, T), :], gn, s.row(5))
            s.col[5:6, :] += jnp.sum(gn * h, axis=0, keepdims=True)
            s.col[6:7, :] += jnp.sum(gn, axis=0, keepdims=True)
            g = g + s.ey[at(i, T), :].astype(f32)
            s.r[at(i, T), :] = g
            e = g.astype(bf16)
            s.er[at(i, T), :] = e
            s.col[4:5, :] += jnp.sum(e.astype(f32), axis=0, keepdims=True)
        loop(s.x.shape[0] // T, body)
    def eA(s):
        def body(i):
            s.n2[:, at(i, T)] = nn(s.er[...], s.OT[:, at(i, T)]).astype(bf16)
        loop(s.x.shape[1] // T, body)
    def attend_back(s, hp):
        L, D = s.x.shape
        q, k, v = s.heads(hp)
        e = s.n2[:, at(hp, 128)]
        kt = k.T
        ea = (e.astype(f32) * s.A[:, at(hp, 128)].astype(f32)).T
        lane = lax.broadcasted_iota(jnp.int32, e.shape, 1)
        s.dk[...] = jnp.zeros_like(s.dk); s.dv[...] = jnp.zeros_like(s.dv)
        for h in (0, 1):
            qh, kh = s.masked(q, k, h)
            mine = (lane // HD) == h
            eh = jnp.where(mine, e, jnp.zeros_like(e))
            qz = jnp.where(mine, q, jnp.zeros_like(q))
            delta = jnp.sum(ea[h * HD:(h + 1) * HD, :], axis=0, keepdims=True)
            for b in range(L // QB):
                cols = slice(b * QB, (b + 1) * QB)
                n = (b + 1) * QB
                parts = s.scores(kh, qh, b)
                lse = s.lse[hp, h:h + 1, cols]
                P = [jnp.exp(p - lse) for p in parts]
                dP = nt(v[:n], eh[cols])
                dl = delta[:, cols]
                dS = [(P[-1] * (dP[n - QB:] - dl)).astype(bf16)]
                if b: dS = [(P[0] * (dP[:n - QB] - dl)).astype(bf16)] + dS
                for i, (p, ds) in enumerate(zip(P, dS)):
                    rows = slice(n - QB, n) if i == len(P) - 1 else slice(0, n - QB)
                    s.dv[rows, :] += nn(p.astype(bf16), eh[cols])
                    s.dk[rows, :] += nn(ds, qz[cols])
                o = nn(kt[h * HD:(h + 1) * HD, n - QB:n], dS[-1])
                if b: o = o + nn(kt[h * HD:(h + 1) * HD, :n - QB], dS[0])
                s.ot[h * HD:(h + 1) * HD, cols] = o * (HD ** -0.5)
        s.u[:, at(hp, 128)] = s.ot[...].T.astype(bf16)
        s.u[:, pl.ds(pl.multiple_of(D + hp * 128, 128), 128)] = s.dk[...].astype(bf16)
        s.u[:, pl.ds(pl.multiple_of(2 * D + hp * 128, 128), 128)] = s.dv[...].astype(bf16)
    def bias_cols(s):
        D = s.x.shape[1]
        def body(i):
            s.col[2:3, :] += jnp.sum(s.u[at(i, T), 0:D].astype(f32), axis=0, keepdims=True)
            s.col[3:4, :] += jnp.sum(s.u[at(i, T), 2 * D:3 * D].astype(f32), axis=0, keepdims=True)
        loop(s.x.shape[0] // T, body)
    def gn1(s):
        D = s.x.shape[1]
        def body(i):
            s.G[:, at(i, T)] = nn(s.u[:, 0:3 * D], s.QT[:, at(i, T)])
        loop(D // T, body)
    def ln1b(s):
        def body(i):
            gn = s.G[at(i, T), :]
            h, g = s.lnb(s.x[at(i, T), :].astype(f32), gn, s.row(0))
            s.col[0:1, :] += jnp.sum(gn * h, axis=0, keepdims=True)
            s.col[1:2, :] += jnp.sum(gn, axis=0, keepdims=True)
            s.er[at(i, T), :] = (s.r[at(i, T), :] + g).astype(bf16)
        loop(s.x.shape[0] // T, body)
    def norm(s):
        t = jnp.sum(s.ssq[...]) + jnp.sum(s.dbf[...] * s.dbf[...]) + jnp.sum(s.col[...] * s.col[...])
        return t

def scratch(L, D, FF, rows=None):
    return dict(
        vec=pltpu.VMEM((8, D), f32), bf=pltpu.VMEM((1, FF), f32), col=pltpu.VMEM((8, D), f32), dbf=pltpu.VMEM((1, FF), f32),
        ssq=pltpu.VMEM((1, 512), f32), kb=pltpu.VMEM((L, 128), bf16),
        n1=pltpu.VMEM((L, D), bf16), m=pltpu.VMEM((L, 3 * D), bf16), A=pltpu.VMEM((L, D), bf16), r=pltpu.VMEM((L, D), f32),
        n2=pltpu.VMEM((L, D), bf16), u=pltpu.VMEM((L, FF), bf16), gp=pltpu.VMEM((L, FF), bf16), er=pltpu.VMEM((L, D), bf16),
        G=pltpu.VMEM((L, D), f32), stage=pltpu.VMEM((2, T, FF), bf16), lt=pltpu.VMEM((T, L), bf16),
        lse=pltpu.VMEM((D // 128, 2, L), f32), ot=pltpu.VMEM((128, L), f32), dk=pltpu.VMEM((L, 128), f32), dv=pltpu.VMEM((L, 128), f32),
        x=pltpu.VMEM((L, D), bf16), ey=pltpu.VMEM((L, D), bf16),
        dsem=pltpu.SemaphoreType.DMA((2,)), isem=pltpu.SemaphoreType.DMA((4,)))


def place():
    d = lax.axis_index("dp"); z = lax.axis_index("fsdp")
    core = d % 2; xx = (d // 2) % 2; yy = d // 4
    return d, z, d + 1 - 2 * core, d + 2 - 4 * xx, d + 4 - 8 * yy


def greet(partners):
    bar = pltpu.get_barrier_semaphore()
    for dev in partners:
        pl.semaphore_signal(bar, inc=1, device_id=dev, device_id_type=MESH)
    pl.semaphore_wait(bar, len(partners))


def split(n):
    return n // 32 * 16 if n >= 32 else n // 2


class Comm:
    def __init__(s):
        s.d, s.z, s.sib, s.xn, s.yn = place()
        s.dg = s.xn + s.yn - s.d
        s.nz = lax.axis_size("fsdp")
        s.partners = [(s.d, (s.z + j) % s.nz) for j in range(1, s.nz)] + [(s.sib, s.z), (s.xn, s.z), (s.yn, s.z)]


class Gather(Comm):
    def __init__(s, items, shards, zb, full, send, recv):
        super().__init__()
        s.items = items; s.sh = shards; s.zb = zb; s.full = full; s.send = send; s.recv = recv
    def cp(s, src, dst, i, slot, dev):
        return pltpu.make_async_remote_copy(src_ref=src, dst_ref=dst, send_sem=s.send.at[i, slot], recv_sem=s.recv.at[i, slot], device_id=dev, device_id_type=MESH)
    def block(s, i, d, half=None):
        w, r0, n = s.items[i]
        ref = s.full[w]
        a, m = (0, n) if half is None else ((0, split(n)) if half == 0 else (split(n), n - split(n)))
        if w == 4:
            return ref.at[d, pl.ds(r0 + a, m)]
        if w == 2:
            cols = ref.shape[1] // 8
            return ref.at[pl.ds(r0 + a, m), pl.ds(pl.multiple_of(d * cols, 128), cols)]
        rows = ref.shape[0] // 8
        return ref.at[pl.ds(pl.multiple_of(d * rows + (r0 + a), 16), m), :]
    def shard(s, i):
        w, r0, n = s.items[i]
        return s.sh[w] if w in (2, 4) else s.sh[w].at[pl.ds(r0, n), :]
    def zslot(s, i, z):
        w, r0, n = s.items[i]
        if w < 2:
            return s.zb[w].at[z, pl.ds(r0, n)]
        ref = s.full[w]
        if w == 2:
            r, c = ref.shape[0] // s.nz, ref.shape[1] // 8
            return ref.at[pl.ds(pl.multiple_of(z * r, 16), r), pl.ds(pl.multiple_of(s.d * c, 128), c)]
        r, c = ref.shape[0] // 8, ref.shape[1] // s.nz
        return ref.at[pl.ds(pl.multiple_of(s.d * r + r0, 16), n), pl.ds(pl.multiple_of(z * c, 128), c)]
    def zc(s, i, j, recv=False):
        other = (s.z - j + s.nz) % s.nz if recv else (s.z + j) % s.nz
        return s.cp(s.shard(i), s.zslot(i, other if recv else s.z), i, j - 1, (s.d, other))
    def start(s, i):
        if s.items[i][0] == 4:
            s.block(i, s.d)[...] = s.shard(i)[...]
            return
        for j in range(1, s.nz):
            s.zc(i, j).start()
        s.zslot(i, s.z)[...] = s.shard(i)[...]
    def sibc(s, i, k, d):
        return s.cp(s.block(i, d), s.block(i, d), i, 7 + k, (s.sib, s.z))
    def bx(s, i, b, dev, slot, half=None):
        return s.cp(s.block(i, b, half), s.block(i, b, half), i, slot, (dev, s.z))
    def e1(s, i):
        w = s.items[i][0]
        if w < 4:
            for j in range(1, s.nz):
                s.zc(i, j, True).wait_recv()
        if w < 2:
            s.block(i, s.d)[...] = jnp.concatenate([s.zslot(i, k)[...] for k in range(s.nz)], axis=1)
        s.bx(i, s.d, s.xn, 3).start()
        s.bx(i, s.d, s.yn, 4).start()
        s.sibc(i, 0, s.d).start()
    def e2(s, i):
        s.bx(i, s.xn, s.xn, 3).wait_recv()
        s.bx(i, s.xn, s.yn, 5, 0).start()
        s.sibc(i, 1, s.xn).start()
    def e3(s, i):
        s.bx(i, s.yn, s.yn, 4).wait_recv()
        s.bx(i, s.yn, s.xn, 6, 1).start()
        s.sibc(i, 2, s.yn).start()
    def e4(s, i):
        s.bx(i, s.dg, s.yn, 5, 0).wait_recv()
        s.bx(i, s.dg, s.xn, 6, 1).wait_recv()
        s.sibc(i, 3, s.dg).start()
    def e5(s, i):
        o = s.sib - s.d
        for k, b in enumerate((s.d, s.xn, s.yn, s.dg)):
            s.sibc(i, k, b + o).wait_recv()
    def finish(s, i):
        if s.items[i][0] < 4:
            for j in range(1, s.nz):
                s.zc(i, j).wait_send()
        s.bx(i, s.d, s.xn, 3).wait_send()
        s.bx(i, s.d, s.yn, 4).wait_send()
        s.bx(i, s.xn, s.yn, 5, 0).wait_send()
        s.bx(i, s.yn, s.xn, 6, 1).wait_send()
        for k, b in enumerate((s.d, s.xn, s.yn, s.dg)):
            s.sibc(i, k, b).wait_send()


class Scatter(Comm):
    def __init__(s, grads, own, sb, ra, rb, rx, ry, zs, zr, out, cs, csem, osem, send, recv):
        super().__init__()
        s.g = grads; s.own = own; s.sb = sb; s.ra = ra; s.rb = rb; s.rx = rx; s.ry = ry; s.zs = zs; s.zr = zr
        s.out = out; s.cs = cs; s.csem = csem; s.osem = osem; s.send = send; s.recv = recv
        s.chips = (s.dg, s.xn, s.yn, s.d)
    def cp(s, src, dst, w, slot, dev):
        return pltpu.make_async_remote_copy(src_ref=src, dst_ref=dst, send_sem=s.send.at[w, slot], recv_sem=s.recv.at[w, slot], device_id=dev, device_id_type=MESH)
    def block(s, w, d):
        ref = s.g[w]
        if w == 4:
            return ref.at[d]
        if w == 2:
            cols = ref.shape[1] // 8
            return ref.at[:, pl.ds(pl.multiple_of(d * cols, 128), cols)]
        rows = ref.shape[0] // 8
        return ref.at[pl.ds(pl.multiple_of(d * rows, 16), rows), :]
    def half(s, ref, h):
        n = ref.shape[0]; k = split(n)
        return ref.at[pl.ds(0, k)] if h == 0 else ref.at[pl.ds(k, n - k)]
    def sibc(s, w, i):
        return s.cp(s.block(w, s.chips[i] + s.sib - s.d), s.sb[w].at[i], w, i, (s.sib, s.z))
    def load(s, w, i):
        return pltpu.make_async_copy(s.block(w, s.chips[i]), s.own[w].at[i], s.osem.at[w, i])
    def cc(s):
        return pltpu.make_async_remote_copy(src_ref=s.cs.at[0], dst_ref=s.cs.at[1], send_sem=s.csem.at[0], recv_sem=s.csem.at[1], device_id=(s.sib, s.z), device_id_type=MESH)
    def s0(s, w):
        for i in range(4):
            s.sibc(w, i).start()
            s.load(w, i).start()
    def ca(s, w): return s.cp(s.half(s.sb[w].at[0], 0), s.ra[w], w, 4, (s.xn, s.z))
    def cb(s, w): return s.cp(s.half(s.sb[w].at[0], 1), s.rb[w], w, 5, (s.yn, s.z))
    def cx(s, w, h): return s.cp(s.half(s.sb[w].at[1], h), s.half(s.rx[w], h), w, 6 + h, (s.xn, s.z))
    def cy(s, w, h): return s.cp(s.half(s.sb[w].at[2], h), s.half(s.ry[w], h), w, 8 + h, (s.yn, s.z))
    def mixed(s, w, i):
        s.sibc(w, i).wait_recv(); s.load(w, i).wait()
        return s.cs[0, 0:1, 0:1] * s.own[w][i].astype(f32) + s.cs[1, 0:1, 0:1] * s.sb[w][i].astype(f32)
    def a(s, w):
        t = s.sb[w]
        t[0] = s.mixed(w, 0).astype(t.dtype); s.ca(w).start(); s.cb(w).start()
        t[1] = s.mixed(w, 1).astype(t.dtype); s.cx(w, 0).start()
        t[2] = s.mixed(w, 2).astype(t.dtype); s.cy(w, 1).start()
    def r(s, w):
        s.ca(w).wait_recv()
        t = s.half(s.sb[w].at[2], 0)
        t[...] = (t[...].astype(f32) + s.ra[w][...].astype(f32)).astype(t.dtype)
        s.cy(w, 0).start()
        s.cb(w).wait_recv()
        t = s.half(s.sb[w].at[1], 1)
        t[...] = (t[...].astype(f32) + s.rb[w][...].astype(f32)).astype(t.dtype)
        s.cx(w, 1).start()
    def zpiece(s, w, k):
        ref = s.zs[w]
        if w in (0, 1): return ref.at[k]
        if w == 4: return ref
        if w == 2:
            r = ref.shape[0] // s.nz
            return ref.at[pl.ds(pl.multiple_of(k * r, 16), r)]
        c = ref.shape[1] // s.nz
        return ref.at[:, pl.ds(pl.multiple_of(k * c, 128), c)]
    def zc(s, w, j):
        to = (s.z + j) % s.nz
        return s.cp(s.zpiece(w, to), s.zr[w].at[j - 1], w, 9 + j, (s.d, to))
    def f(s, w):
        t = s.mixed(w, 3)
        for h in (0, 1):
            s.cx(w, h).wait_recv(); s.cy(w, h).wait_recv()
        t = t + s.rx[w][...].astype(f32) + s.ry[w][...].astype(f32)
        if w in (0, 1):
            c = t.shape[1] // s.nz
            for k in range(s.nz): s.zs[w][k] = t[:, k * c:(k + 1) * c].astype(bf16)
        else:
            s.zs[w][...] = t.astype(s.zs[w].dtype)
        for j in range(1, s.nz): s.zc(w, j).start()
    def zf(s, w):
        for j in range(1, s.nz): s.zc(w, j).wait_recv()
        t = s.zpiece(w, s.z)[...].astype(f32)
        for j in range(s.nz - 1): t = t + s.zr[w][j].astype(f32)
        s.out[w][...] = t
    def finish(s, w):
        for i in range(4): s.sibc(w, i).wait_send()
        s.ca(w).wait_send(); s.cb(w).wait_send()
        for h in (0, 1): s.cx(w, h).wait_send(); s.cy(w, h).wait_send()
        for j in range(1, s.nz): s.zc(w, j).wait_send()


def rs_kernel(c, *refs):
    refs = list(refs)
    take = lambda n: [refs.pop(0) for _ in range(n)]
    grads = take(5); outs = take(5)
    parts = [take(5) for _ in range(8)]
    s = Scatter(grads, *parts, outs, *refs)
    greet(s.partners)
    q, o, f, p, v = range(5)
    for w in (o, v, q, f, p): s.s0(w)
    s.cs[0] = jnp.full(s.cs.shape[1:], c[0], f32)
    s.cc().start(); s.cc().wait_recv()
    s.a(o); s.a(v); s.a(q); s.r(o); s.r(v); s.a(f); s.r(q); s.f(o); s.f(v); s.a(p); s.r(f); s.f(q); s.r(p); s.f(f)
    s.zf(o); s.zf(v); s.zf(q); s.f(p); s.zf(f); s.zf(p)
    s.cc().wait_send()
    for w in range(5): s.finish(w)


def scatter_all(c, gq, go, gf, gp, gv):
    nz = lax.axis_size("fsdp")
    grads = (gq, go, gf, gp, gv)
    blocks = [(gq.shape[0] // 8, gq.shape[1]), (go.shape[0] // 8, go.shape[1]), (gf.shape[0], gf.shape[1] // 8), (gp.shape[0] // 8, gp.shape[1]), gv.shape[1:]]
    dt = [bf16] * 4 + [f32]
    ha = [(split(r), c_) for r, c_ in blocks]
    hb = [(r - split(r), c_) for r, c_ in blocks]
    piece = [(r, c_ // nz) for r, c_ in blocks[:2]] + [(blocks[2][0] // nz, blocks[2][1]), (blocks[3][0], blocks[3][1] // nz), blocks[4]]
    zs = [(nz,) + piece[0], (nz,) + piece[1]] + blocks[2:]
    zr = [(nz - 1,) + s for s in piece]
    V = lambda ss: [pltpu.VMEM(s, t) for s, t in zip(ss, dt)]
    four = [(4,) + b for b in blocks]
    vm = pl.BlockSpec(memory_space=pltpu.VMEM)
    an = pl.BlockSpec(memory_space=pl.ANY)
    dma = pltpu.SemaphoreType.DMA
    return pl.pallas_call(rs_kernel, out_shape=[jax.ShapeDtypeStruct(s, f32) for s in piece],
        in_specs=[pl.BlockSpec(memory_space=pltpu.SMEM)] + [an] * 5, out_specs=[vm] * 5,
        scratch_shapes=V(four) + V(four) + V(ha) + V(hb) + V(blocks) + V(blocks) + V(zs) + V(zr)
            + [pltpu.VMEM((2, 8, 128), f32), dma((2,)), dma((5, 4)), dma((5, 13)), dma((5, 13))],
        compiler_params=pltpu.CompilerParams(collective_id=1, has_side_effects=True, vmem_limit_bytes=60 << 20))(c, *grads)


def block_kernel(names, remote, length, tok, cot, *refs):
    refs = list(refs)
    take = lambda n: [refs.pop(0) for _ in range(n)]
    if remote:
        raw = take(5)
        y, gx, gq, go, gf, gp, gv, ss = take(8)
        QT, OT, F, PT, V, sq, so, sf, sp, zq, zo, send, recv = take(13)
    else:
        QT, OT, F, PT, vec, bf = take(6)
        y, gx, gq, go, gf, gp, col, dbf, ss = take(9)
        V = None
    s = Block(length=length[0], QT=QT, OT=OT, F=F, PT=PT, V=V, **dict(zip(names, refs)))
    D = s.x.shape[1]; FF = s.u.shape[1]
    cx = pltpu.make_async_copy(tok, s.x, s.isem.at[0]); cx.start()
    ce = pltpu.make_async_copy(cot, s.ey, s.isem.at[1]); ce.start()
    if remote:
        rows = sq.shape[0]
        items = [(4, 0, 16), (0, 0, rows // 2), (0, rows // 2, rows - rows // 2), (1, 0, so.shape[0]), (2, 0, F.shape[0]), (3, 0, sp.shape[0])]
        g = Gather(items, (sq, so, sf, sp, raw[4]), (zq, zo), (QT, OT, F, PT, V), send, recv)
        sq[...] = raw[0][...].astype(bf16).T
        so[...] = raw[1][...].astype(bf16).T
        sf[...] = raw[2][...].astype(bf16)
        sp[...] = raw[3][...].astype(bf16).T
        greet(g.partners)
        v, q1, q2, o, f, p = range(6)
        for i in range(6): g.start(i)
        g.e1(v); g.e2(v); g.e3(v); g.e4(v)
        g.e1(q1); g.e5(v); s.unpack(); cx.wait(); s.ln1()
        g.e1(q2); g.e2(q1); g.e3(q1); g.e1(o); g.e2(q2); g.e3(q2); g.e4(q1); g.e1(f); g.e2(o); g.e3(o); g.e4(q2)
        g.e5(q1); g.e5(q2)
        s.qkv()
        def pair(hp):
            @pl.when(hp == 0)
            def _(): g.e4(o); g.e1(p)
            @pl.when(hp == 3)
            def _(): g.e2(f); g.e3(f)
            s.attend(hp)
        loop(D // 128, pair)
        g.e4(f); g.e5(o)
        s.out(); s.ln2(); g.e2(p); g.e3(p); g.e5(f); s.fc()
    else:
        s.vec[...] = vec[...]; s.bf[...] = bf[...]
        s.clear(); cx.wait()
        s.ln1(); s.qkv()
        loop(D // 128, s.attend)
        s.out(); s.ln2(); s.fc()
    ce.wait(); s.ey_mask()
    if remote: g.e4(p)
    s.wgrad(s.ey, s.u, gp, 512, FF)
    if remote: g.e5(p)
    s.y()
    cy = pltpu.make_async_copy(s.er, y, s.isem.at[2]); cy.start()
    s.ef(); s.wgrad(s.n2, s.gp, gf, 512, FF); s.gn2()
    cy.wait()
    s.ln2b(); s.wgrad(s.er, s.A, go, 256, D); s.eA()
    loop(D // 128, s.attend_back)
    s.bias_cols(); s.gn1(); s.ln1b()
    cg = pltpu.make_async_copy(s.er, gx, s.isem.at[3]); cg.start()
    s.wgrad(s.u, s.n1, gq, 256, D)
    cg.wait()
    ss[0] = s.norm()
    if remote:
        w = D // 8; nb = FF // 8 // 128
        for d in range(8):
            gv[d, 0:8, 0:w] = s.col[:, d * w:(d + 1) * w]
            gv[d, 0:8, w:128] = jnp.zeros((8, 128 - w), f32)
            for j in range(8):
                k = d * nb + j
                gv[d, 8 + j:9 + j, :] = s.dbf[:, k * 128:(k + 1) * 128] if j < nb else jnp.zeros((1, 128), f32)
        for i in range(6): g.finish(i)
    else:
        col[...] = s.col[...]; dbf[...] = s.dbf[...]


def run_block(remote, length, tok, cot, *ws):
    L, D = tok.shape
    sd = jax.ShapeDtypeStruct
    dma = pltpu.SemaphoreType.DMA
    vm = pl.BlockSpec(memory_space=pltpu.VMEM); an = pl.BlockSpec(memory_space=pl.ANY); sm = pl.BlockSpec(memory_space=pltpu.SMEM)
    extra = []
    if remote:
        nz = lax.axis_size("fsdp")
        q, o, f, p, v = ws
        FF = f.shape[1] * 8
        qt, ot, pt = q.shape[::-1], o.shape[::-1], p.shape[::-1]
        extra = [pltpu.VMEM((3 * D, D), bf16), pltpu.VMEM((D, D), bf16), pltpu.VMEM((D, FF), bf16), pltpu.VMEM((D, FF), bf16), pltpu.VMEM((8,) + v.shape, f32),
            pltpu.VMEM(qt, bf16), pltpu.VMEM(ot, bf16), pltpu.VMEM(f.shape, bf16), pltpu.VMEM(pt, bf16),
            pltpu.VMEM((nz,) + qt, bf16), pltpu.VMEM((nz,) + ot, bf16), dma((6, 11)), dma((6, 11))]
        tail = [sd((8,) + v.shape, f32)]
    else:
        FF = ws[2].shape[1]
        tail = [sd((8, D), f32), sd((1, FF), f32)]
    scr = scratch(L, D, FF)
    params = dict(collective_id=0, has_side_effects=True) if remote else {}
    return pl.pallas_call(functools.partial(block_kernel, list(scr), remote),
        out_shape=[sd((L, D), bf16), sd((L, D), bf16), sd((3 * D, D), bf16), sd((D, D), bf16), sd((D, FF), bf16), sd((D, FF), bf16)] + tail + [sd((1,), f32)],
        in_specs=[sm, an, an] + [vm] * len(ws), out_specs=[an] * 6 + [vm] * len(tail) + [sm], scratch_shapes=extra + list(scr.values()),
        compiler_params=pltpu.CompilerParams(vmem_limit_bytes=VLIM, **params))(length, tok, cot, *ws)


VLIM = 63 << 20


def shards(tokens, qkv_weight, out_weight, fc_weight, proj_weight, fc_bias, vectors, cotangent, lengths, clip_norm,
           noise_qkv, noise_out, noise_fc, noise_proj, noise_fc_bias, noise_vectors):
    ndp, nz = lax.axis_size("dp"), lax.axis_size("fsdp")
    if ndp == 8:
        nb = fc_bias.shape[0] // 128
        small = jnp.concatenate([jnp.pad(vectors, ((0, 0), (0, 128 - vectors.shape[1]))), jnp.pad(fc_bias.reshape(nb, 128), ((0, 8 - nb), (0, 0)))], axis=0)
        y, gx, gq, go, gf, gp, gv, ss = run_block(True, lengths, tokens, cotangent, qkv_weight, out_weight, fc_weight, proj_weight, small)
    else:
        g = lambda a: lax.all_gather(lax.all_gather(a.astype(bf16), "dp", axis=1, tiled=True), "fsdp", axis=0, tiled=True)
        vec = lax.all_gather(vectors.astype(bf16), "dp", axis=1, tiled=True).astype(f32)
        bf = lax.all_gather(fc_bias.astype(bf16), "dp", axis=0, tiled=True).astype(f32).reshape(1, -1)
        y, gx, gq, go, gf, gp, col, dbf, ss = run_block(False, lengths, tokens, cotangent, g(qkv_weight).T, g(out_weight).T, g(fc_weight), g(proj_weight).T, vec, bf)
    norm = jnp.sqrt(ss)
    factor = jnp.minimum(1.0, clip_norm / norm)
    if ndp == 8:
        sq, so, sf, sp, sv = scatter_all(factor, gq, go, gf, gp, gv)
        finals = (sq.T, so.T, sf, sp.T, sv[8:8 + nb].reshape(-1), sv[:8, :vectors.shape[1]])
    else:
        ps = lambda a, dim: lax.psum_scatter(factor * a.astype(f32), "dp", scatter_dimension=dim, tiled=True)
        pz = lambda a: lax.psum_scatter(a.astype(bf16), "fsdp", scatter_dimension=0, tiled=True).astype(f32)
        finals = tuple(pz(ps(a, 1)) for a in (gq.T, go.T, gf, gp.T)) + lax.psum((ps(dbf[0], 0), ps(col, 1)), "fsdp")
    examples = ndp * nz
    noises = (noise_qkv, noise_out, noise_fc, noise_proj, noise_fc_bias, noise_vectors)
    return (y, gx, norm / clip_norm) + tuple(a / examples + n for a, n in zip(finals, noises))


def solution(mesh):
    both, cut = P(("dp", "fsdp"), None), P("fsdp", "dp")
    weights = (cut, cut, cut, cut, P("dp"), P(None, "dp"))
    return jax.shard_map(shards, mesh=mesh, in_specs=(both,) + weights + (both, P(("dp", "fsdp")), P()) + weights,
        out_specs=(both, both, P(("dp", "fsdp"))) + weights, check_vma=False)
```

time: 991 us -> 286 us (0.29)
  waiting for transfers between devices: 446 us -> 0 us
  Pallas kernels: 0 us -> 269 us
  matrix products: 241 us -> 0 us
  other arithmetic: 127 us -> 6.47 us
  blocking collectives: 76.6 us -> 0 us
  local copies, waits for them, and re-layouts: 71.3 us -> 6.87 us
  between operations: 22.1 us -> 3.96 us
    pallas_call x0 -> x2, Pallas kernels: none -> 269 us  [the longest x1 182 us: run_block(): pl.pallas_call(functools.partial(block_kernel, list(scr), remote), out_sh...]
    dot_general x24 -> x0, matrix products: 241 us -> none  [the longest x2 40.8 us: attend_back(): jnp.einsum('qhd,khd->hqk', grad_block, value_rows, preferred_element_type...]
    all_gather x6 -> x0, waiting for transfers between devices: 159 us -> none  [the longest x1 71.8 us: shards(): lax.all_gather(attn_cols[0], 'fsdp', axis=0, tiled=True)]
    unnamed x19 -> x0, waiting for transfers between devices: 150 us -> none
    reduce_scatter x5 -> x0, waiting for transfers between devices: 137 us -> none  [the longest x1 64 us: shards(): lax.psum_scatter(weighted[2], 'dp', scatter_dimension=1, tiled=True)]
    convert_element_type x8 -> x0, other arithmetic: 50.9 us -> none  [the longest x1 42.5 us: attend_back(): grad_scores = (chances * (grad_chances - inner)).astype(jnp.bfloat16)]
    unnamed x139 -> x29, local copies, waits for them, and re-layouts: 54.3 us -> 6.87 us
    all_gather x4 -> x0, blocking collectives: 41.7 us -> none  [the longest x1 14.5 us: shards(): lax.all_gather(low_qkv, 'dp', axis=1, tiled=True)]
  transfers between devices with their start and end apart: 15 -> 0, of which waited for: 11 -> 0; matrix products, arithmetic and copies ran while one was open for 20% -> 0% of each run, Pallas kernels for 0% -> 0%
where the time goes in v2:
time: 286 us
  Pallas kernels  269 us (94%)
  local copies, waits for them, and re-layouts  6.87 us (2%)
  other arithmetic  6.47 us (2%)
  between operations  3.96 us (1%)
    pallas_call x1, Pallas kernels, run_block(): pl.pallas_call(functools.partial(block_kernel, list(scr), remote), out_sh...  182 us
    pallas_call x1, Pallas kernels, scatter_all(): pl.pallas_call(rs_kernel, out_shape=[jax.ShapeDtypeStruct(s, f32) for s i...  86.7 us
    unnamed x29, local copies, waits for them, and re-layouts  6.87 us

profile of v2, /device:TPU:0, one launch (start us, length us, event | category | flops | bytes accessed | tf_op | source)
XLA Modules:
  0.0 286.0 jit_solution(6077661276828321108)
XLA Ops:
  0.6 1.9 copy.25.refs_3_
  2.5 1.3 select_maximum_fusion.refs_4_
  4.5 182.0 %shard_map.223 = (bf16[1024,768]{1,0:T(8,128)(2,1)}, bf16[1024,768]{1,0:T(8,128)(2,1)}, bf16[2304,768]{1,0:T(8,128)(2,1)}, bf16[768,768]{1,0:T(8,128)(2,1)}, bf1...) custom-call(s32[1]{0:T(128)S(6)} %copy.32.length, ...), custom_call_target="tpu_custom_call" | custom-call | tf_op jit(solution)/shard_map/pallas_call | solution.py:568
  187.9 0.0 copy-start.9
  187.9 0.0 copy-start.10
  187.9 0.0 copy-start.6
  187.9 86.7 %shard_map.224 = (f32[288,192]{1,0:T(8,128)}, f32[96,192]{1,0:T(8,128)}, f32[192,384]{1,0:T(8,128)}, f32[96,768]{1,0:T(8,128)}, f32[16,128]{1,0:T(8,128)}) custom-call(f32[1]{0:T(128)S(6)} %min.3.c, bf16[2304,768]{1,0:T(8,128)(2,1)} %get-tuple-element.25.refs_0_, bf16[768,768]{1,0:T(8,128)(2,1)} %get-tuple-element.26.refs_1_, ...), custom_call_target="tpu_custom_call" | custom-call | tf_op jit(solution)/shard_map/pallas_call | solution.py:467
  274.6 0.0 copy-start.2
  274.6 0.0 copy-start.5
  274.6 0.0 copy-start.7
  274.6 0.0 copy-done.9
  274.6 1.3 multiply_add_fusion.1
  275.9 0.0 copy-done.10
  275.9 1.3 bitcast_add_fusion.3
  277.2 0.0 copy-done.6
  277.2 0.0 copy-start.8
  277.2 0.1 copy.26
  277.3 0.0 copy-start.3
  277.4 0.0 copy-start.4
  277.4 1.1 bitcast_add_fusion.1
  278.4 0.0 copy-start.1
  278.4 0.9 copy.28
  279.3 0.0 copy-done.2
  279.3 0.0 copy-done.5
  279.3 0.7 bitcast_add_fusion
  280.1 0.0 copy-done.7
  280.1 0.1 copy.27
  280.2 0.0 copy-done.8
  280.2 0.7 copy.29
  280.9 0.0 copy-done.3
  280.9 0.0 copy-done.4
  280.9 0.7 multiply_add_fusion
  281.7 0.0 copy-done.1
  281.7 0.0 copy-start
  281.7 1.1 copy.34
  282.9 0.8 copy-done
  283.7 1.1 copy.35
  (1 shorter events, 0.0 us)
Async XLA Ops:
  187.9 86.7 %copy-start.9 = (f32[8,96]{1,0:T(8,128)S(1)}, f32[8,96]{1,0:T(8,128)}, u32[]{:S(2)}) copy-start(f32[8,96]{1,0:T(8,128)} %param.31) | copy-start | bytes 9220
  187.9 88.1 %copy-start.10 = (f32[384]{0:T(512)S(1)}, f32[384]{0:T(512)}, u32[]{:S(2)}) copy-start(f32[384]{0:T(512)} %param.30) | copy-start | bytes 4612
  187.9 89.3 %copy-start.6 = (f32[192,288]{1,0:T(8,128)S(1)}, f32[192,288]{1,0:T(8,128)}, u32[]{:S(2)}) copy-start(f32[192,288]{1,0:T(8,128)} %param.26) | copy-start | bytes 663556
  274.6 4.8 %copy-start.2 = (f32[768,96]{0,1:T(8,128)S(1)}, f32[768,96]{0,1:T(8,128)}, u32[]{:S(2)}) copy-start(f32[768,96]{0,1:T(8,128)} %param.29) | copy-start | bytes 884740
  274.6 4.7 %copy-start.5 = (f32[96,768]{1,0:T(8,128)S(1)}, f32[96,768]{1,0:T(8,128)}, u32[]{:S(2)}) copy-start(f32[96,768]{1,0:T(8,128)} %get-tuple-element.33) | copy-start | bytes 884740
  274.6 5.5 %copy-start.7 = (f32[192,96]{1,0:T(8,128)S(1)}, f32[192,96]{1,0:T(8,128)}, u32[]{:S(2)}) copy-start(f32[192,96]{1,0:T(8,128)} %param.27) | copy-start | bytes 221188
  277.2 3.0 %copy-start.8 = (f32[96,192]{1,0:T(8,128)S(1)}, f32[96,192]{1,0:T(8,128)}, u32[]{:S(2)}) copy-start(f32[96,192]{1,0:T(8,128)} %get-tuple-element.31) | copy-start | bytes 221188
  277.3 3.6 %copy-start.3 = (f32[192,384]{1,0:T(8,128)S(1)}, f32[192,384]{1,0:T(8,128)}, u32[]{:S(2)}) copy-start(f32[192,384]{1,0:T(8,128)} %param.28) | copy-start | bytes 884740
  277.4 3.6 %copy-start.4 = (f32[192,384]{1,0:T(8,128)S(1)}, f32[192,384]{1,0:T(8,128)}, u32[]{:S(2)}) copy-start(f32[192,384]{1,0:T(8,128)} %get-tuple-element.32) | copy-start | bytes 884740
  278.4 3.3 %copy-start.1 = (bf16[1024,768]{1,0:T(8,128)(2,1)S(1)}, bf16[1024,768]{1,0:T(8,128)(2,1)}, u32[]{:S(2)}) copy-start(bf16[1024,768]{1,0:T(8,128)(2,1)} %get-tuple-element.53) | copy-start | bytes 4718596
  281.7 2.0 copy-start

commit v3 on v2

--- a/solution.py
+++ b/solution.py
@@ -1,4 +1,5 @@
 import functools
+import types
 import jax
 import jax.numpy as jnp
 from jax import lax
@@ -116,21 +117,23 @@
             s.col[7:8, :] += jnp.sum(e, axis=0, keepdims=True)
         loop(s.x.shape[0] // T, body)
     def wgrad(s, lhs, rhs, out, nw, cols, first=0):
-        N = cols; M = out.shape[0]
-        def cp(i): return pltpu.make_async_copy(s.stage.at[i % 2, :, pl.ds(0, N)], out.at[at(i, T), :], s.dsem.at[i % 2])
+        W = min(cols, s.stage.shape[2]); nh = cols // W; n = out.shape[0] // T
+        def cp(i, h):
+            slot = (i * nh + h) % 2
+            return pltpu.make_async_copy(s.stage.at[slot, :, pl.ds(0, W)], out.at[at(i, T), pl.ds(h * W, W)], s.dsem.at[slot])
         def body(i):
             s.lt[...] = lhs[:, at(i, T)].T
-            @pl.when(i >= 2)
-            def _(): cp(i - 2).wait()
-            def inner(j):
-                o = nn(s.lt[...], rhs[:, at(j, nw)])
-                s.ssq[:, 0:nw] += jnp.sum(o * o, axis=0, keepdims=True)
-                s.stage[i % 2, :, at(j, nw)] = o.astype(bf16)
-            loop(N // nw, inner)
-            cp(i).start()
-        n = M // T
+            for h in range(nh):
+                @pl.when(i * nh + h >= 2)
+                def _(): cp(i - 2 // nh, h).wait()
+                def inner(j):
+                    o = nn(s.lt[...], rhs[:, pl.ds(pl.multiple_of(h * W + j * nw, nw), nw)])
+                    s.ssq[:, 0:nw] += jnp.sum(o * o, axis=0, keepdims=True)
+                    s.stage[(i * nh + h) % 2, :, at(j, nw)] = o.astype(bf16)
+                loop(W // nw, inner)
+                cp(i, h).start()
         loop(n, body)
-        cp(n - 2).wait(); cp(n - 1).wait()
+        for t in (n * nh - 2, n * nh - 1): cp(t // nh, t % nh).wait()
     def y(s):
         def body(i):
             o = nt(s.u[...], s.PT[at(i, T), :])
@@ -233,7 +236,7 @@
         ssq=pltpu.VMEM((1, 512), f32), kb=pltpu.VMEM((L, 128), bf16),
         n1=pltpu.VMEM((L, D), bf16), m=pltpu.VMEM((L, 3 * D), bf16), A=pltpu.VMEM((L, D), bf16), r=pltpu.VMEM((L, D), f32),
         n2=pltpu.VMEM((L, D), bf16), u=pltpu.VMEM((L, FF), bf16), gp=pltpu.VMEM((L, FF), bf16), er=pltpu.VMEM((L, D), bf16),
-        G=pltpu.VMEM((L, D), f32), stage=pltpu.VMEM((2, T, FF), bf16), lt=pltpu.VMEM((T, L), bf16),
+        G=pltpu.VMEM((L, D), f32), stage=pltpu.VMEM((2, T, FF // 2), bf16), lt=pltpu.VMEM((T, L), bf16),
         lse=pltpu.VMEM((D // 128, 2, L), f32), ot=pltpu.VMEM((128, L), f32), dk=pltpu.VMEM((L, 128), f32), dv=pltpu.VMEM((L, 128), f32),
         x=pltpu.VMEM((L, D), bf16), ey=pltpu.VMEM((L, D), bf16),
         dsem=pltpu.SemaphoreType.DMA((2,)), isem=pltpu.SemaphoreType.DMA((4,)))
@@ -261,7 +264,7 @@
         s.d, s.z, s.sib, s.xn, s.yn = place()
         s.dg = s.xn + s.yn - s.d
         s.nz = lax.axis_size("fsdp")
-        s.partners = [(s.d, (s.z + j) % s.nz) for j in range(1, s.nz)] + [(s.sib, s.z), (s.xn, s.z), (s.yn, s.z)]
+        s.partners = [(s.d, (s.z + j) % s.nz) for j in range(1, s.nz)] + [((s.d + k) % 8, s.z) for k in range(1, 8)]
 
 
 class Gather(Comm):
@@ -346,138 +349,225 @@
             s.sibc(i, k, b).wait_send()
 
 
-class Scatter(Comm):
-    def __init__(s, grads, own, sb, ra, rb, rx, ry, zs, zr, out, cs, csem, osem, send, recv):
+class Reduce(Comm):
+    def __init__(s, hbm, far, near, v, sems):
         super().__init__()
-        s.g = grads; s.own = own; s.sb = sb; s.ra = ra; s.rb = rb; s.rx = rx; s.ry = ry; s.zs = zs; s.zr = zr
-        s.out = out; s.cs = cs; s.csem = csem; s.osem = osem; s.send = send; s.recv = recv
+        s.hbm = hbm; s.v = v; s.near = near
+        s.pP, s.pF = far
+        s.sems = sems
         s.chips = (s.dg, s.xn, s.yn, s.d)
-    def cp(s, src, dst, w, slot, dev):
-        return pltpu.make_async_remote_copy(src_ref=src, dst_ref=dst, send_sem=s.send.at[w, slot], recv_sem=s.recv.at[w, slot], device_id=dev, device_id_type=MESH)
-    def block(s, w, d):
-        ref = s.g[w]
+        s.ndp = 8
+        s.fr = hbm[2].shape[0] // s.nz; s.fh = s.fr // 2; s.fc = hbm[2].shape[1] // 8
+        s.qr = hbm[0].shape[0] // 8; s.orr = hbm[1].shape[0] // 8; s.pr = hbm[3].shape[0] // 8; s.pc = hbm[3].shape[1] // s.nz
+        s.peers = [((s.d + k) % 8, s.z) for k in range(1, 8)] + [(s.d, (s.z + j) % s.nz) for j in range(1, s.nz)]
+    def cp(s, src, dst, kind, i, dev):
+        a, b = s.sems[kind]
+        return pltpu.make_async_remote_copy(src_ref=src, dst_ref=dst, send_sem=a.at[i], recv_sem=b.at[i], device_id=dev, device_id_type=MESH)
+    def rows(s, ref, d, n): return ref.at[pl.ds(pl.multiple_of(d * n, 16), n), :]
+    def pp(s, k):
+        d = (s.d + k) % 8
+        return s.cp(s.rows(s.hbm[3], d, s.pr), s.pP.at[k - 1], "p", k - 1, (d, s.z))
+    def start_p(s):
+        for k in (2, 6, 4, 3, 5, 7, 1): s.pp(k).start()
+    def pf(s, j):
+        z = (s.z + j) % s.nz
+        return s.cp(s.hbm[2].at[pl.ds(pl.multiple_of(z * s.fr, 16), s.fh), :], s.pF.at[j - 1], "f", j - 1, (s.d, z))
+    def start_f(s):
+        for j in range(1, s.nz): s.pf(j).start()
+    def fpiece(s, d, k):
+        return s.hbm[2].at[pl.ds(k * s.fr + s.fh, s.fh), pl.ds(pl.multiple_of(d * s.fc, 128), s.fc)]
+    def s0(s, w, i, k=0):
+        d = s.chips[i] + s.sib - s.d
+        if w == 2:
+            return s.cp(s.fpiece(d, k), s.near[2].at[i, pl.ds(k * s.fh, s.fh)], "s", w * 4 + i, (s.sib, s.z))
+        return s.cp(s.rows(s.hbm[w], d, s.qr if w == 0 else s.orr), s.near[w].at[i], "s", w * 4 + i, (s.sib, s.z))
+    def s0all(s, w, i): return s.cp(s.near[w].at[i], s.near[w].at[i], "s", w * 4 + i, (s.sib, s.z))
+    def start_s(s, w):
+        for i in range(4):
+            for k in range(s.nz if w == 2 else 1): s.s0(w, i, k).start()
+    def own(s, w, i):
+        v = s.v
+        if w == 0: return v.QT.at[pl.ds(i * s.qr, s.qr)]
+        if w == 1: return v.OT.at[pl.ds(i * s.orr, s.orr)]
+        if w == 2: return v.F.at[pl.ds(0, s.nz * s.fh), pl.ds(i * s.fc, s.fc)]
+        if w == 3: return v.gp.at[pl.ds(512, s.fh), pl.ds(pl.multiple_of(s.chips[i] * s.fc, 128), s.fc)]
+        return v.gv.at[s.chips[i]]
+    def sb(s, w, i):
+        v = s.v
+        if w == 0: return v.QT.at[pl.ds((4 + i) * s.qr, s.qr)]
+        if w == 1: return v.OT.at[pl.ds((4 + i) * s.orr, s.orr)]
+        if w == 2: return v.F.at[pl.ds(0, s.nz * s.fh), pl.ds((4 + i) * s.fc, s.fc)]
+        if w == 3: return v.gp.at[pl.ds(512 + s.fh, s.fh), pl.ds(i * s.fc, s.fc)]
+        return v.vs.at[i]
+    def land(s, w, what):
+        v = s.v
+        i = ("rx", "ry", "ra", "rb", "zs").index(what)
+        if w == 2 or w == 3:
+            ref, base, n = (v.F, s.nz * s.fh, s.nz * s.fh) if w == 2 else (v.gp, 512 + 2 * s.fh, s.fh)
+            k = split(n)
+            a, m, c = [(0, n, 0), (0, n, 1), (0, k, 2), (k, n - k, 2), (0, n, 3)][i]
+            return ref.at[pl.ds(base + a, m), pl.ds(c * s.fc, s.fc)]
         if w == 4:
-            return ref.at[d]
-        if w == 2:
-            cols = ref.shape[1] // 8
-            return ref.at[:, pl.ds(pl.multiple_of(d * cols, 128), cols)]
-        rows = ref.shape[0] // 8
-        return ref.at[pl.ds(pl.multiple_of(d * rows, 16), rows), :]
+            return [v.vs.at[4], v.vs.at[5], v.vs.at[6, pl.ds(0, 8)], v.vs.at[6, pl.ds(8, 8)], v.vs.at[7]][i]
+        ref, n = (v.n1, s.qr) if w == 0 else (v.A, s.orr)
+        if what == "zs": return (v.zq, v.zo)[w]
+        k = split(n)
+        a, m = [(0, n), (n, n), (2 * n, k), (2 * n + k, n - k)][i]
+        return ref.at[pl.ds(a, m)]
     def half(s, ref, h):
         n = ref.shape[0]; k = split(n)
         return ref.at[pl.ds(0, k)] if h == 0 else ref.at[pl.ds(k, n - k)]
-    def sibc(s, w, i):
-        return s.cp(s.block(w, s.chips[i] + s.sib - s.d), s.sb[w].at[i], w, i, (s.sib, s.z))
-    def load(s, w, i):
-        return pltpu.make_async_copy(s.block(w, s.chips[i]), s.own[w].at[i], s.osem.at[w, i])
-    def cc(s):
-        return pltpu.make_async_remote_copy(src_ref=s.cs.at[0], dst_ref=s.cs.at[1], send_sem=s.csem.at[0], recv_sem=s.csem.at[1], device_id=(s.sib, s.z), device_id_type=MESH)
-    def s0(s, w):
+    def ld(s, w, i, k=0):
+        src = s.fpiece(s.chips[i], k) if w == 2 else s.rows(s.hbm[w], s.chips[i], s.qr if w == 0 else s.orr)
+        dst = s.own(2, i).at[pl.ds(k * s.fh, s.fh)] if w == 2 else s.own(w, i)
+        return pltpu.make_async_copy(src, dst, s.v.lsem.at[w * 8 + i])
+    def lds(s, w, i): return pltpu.make_async_copy(s.near[w].at[i], s.sb(w, i), s.v.lsem.at[w * 8 + 4 + i])
+    def load_own(s, w):
         for i in range(4):
-            s.sibc(w, i).start()
-            s.load(w, i).start()
-    def ca(s, w): return s.cp(s.half(s.sb[w].at[0], 0), s.ra[w], w, 4, (s.xn, s.z))
-    def cb(s, w): return s.cp(s.half(s.sb[w].at[0], 1), s.rb[w], w, 5, (s.yn, s.z))
-    def cx(s, w, h): return s.cp(s.half(s.sb[w].at[1], h), s.half(s.rx[w], h), w, 6 + h, (s.xn, s.z))
-    def cy(s, w, h): return s.cp(s.half(s.sb[w].at[2], h), s.half(s.ry[w], h), w, 8 + h, (s.yn, s.z))
+            for k in range(s.nz if w == 2 else 1): s.ld(w, i, k).start()
+    def load_sib(s, w):
+        for i in range(4):
+            s.s0all(w, i).wait_recv()
+            s.lds(w, i).start()
+    def lp(s, k):
+        src = s.rows(s.hbm[3], s.d, s.pr) if k == 0 else s.pP.at[k - 1]
+        return pltpu.make_async_copy(src, s.v.PT.at[pl.ds(k * s.pr, s.pr)], s.v.lsem.at[24 + k])
+    def load_p(s):
+        for k in range(8):
+            if k: s.pp(k).wait_recv()
+            s.lp(k).start()
+    def lf(s, j):
+        src = s.hbm[2].at[pl.ds(pl.multiple_of(s.z * s.fr, 16), s.fh), :] if j == 0 else s.pF.at[j - 1]
+        return pltpu.make_async_copy(src, s.v.gp.at[pl.ds(j * s.fh, s.fh)], s.v.lsem.at[32 + j])
+    def load_f(s):
+        for j in range(s.nz):
+            if j: s.pf(j).wait_recv()
+            s.lf(j).start()
+    def cc(s, i): return s.cp(s.v.cs.at[0], s.v.cs.at[1 + i], "c", i, s.peers[i])
+    def factors(s, c):
+        s.v.cs[0] = jnp.full(s.v.cs.shape[1:], c, f32)
+        for i in range(len(s.peers)): s.cc(i).start()
+    def wait_factors(s):
+        for i in range(len(s.peers)): s.cc(i).wait_recv()
+    def c(s, i): return s.v.cs[i, 0:1, 0:1]
+    def sibv(s, w, i):
+        src = s.v.gv.at[s.chips[i] + s.sib - s.d] if w == 4 else s.v.gp.at[pl.ds(512, s.fh), pl.ds(pl.multiple_of((s.chips[i] + s.sib - s.d) * s.fc, 128), s.fc)]
+        return s.cp(src, s.sb(w, i), "n", w * 13 + i, (s.sib, s.z))
+    def start_v(s, w):
+        for i in range(4): s.sibv(w, i).start()
+    def psum(s):
+        for k in range(8): s.lp(k).wait()
+        n = s.pr
+        for q in range(s.nz):
+            t = s.c(0) * s.v.PT[0:n, q * s.pc:(q + 1) * s.pc].astype(f32)
+            for k in range(1, 8): t = t + s.c(k) * s.v.PT[k * n:(k + 1) * n, q * s.pc:(q + 1) * s.pc].astype(f32)
+            s.v.gp[800:800 + n, q * s.pc:(q + 1) * s.pc] = t.astype(bf16)
+        for j in range(1, s.nz): s.pz(j).start()
+    def pz(s, j):
+        z = (s.z + j) % s.nz
+        return s.cp(s.v.gp.at[pl.ds(800, s.pr), pl.ds(pl.multiple_of(z * s.pc, 128), s.pc)],
+            s.v.gp.at[pl.ds(896, s.pr), pl.ds((j - 1) * s.pc, s.pc)], "z", j - 1, (s.d, z))
+    def pfin(s):
+        for j in range(1, s.nz): s.pz(j).wait_recv()
+        t = s.v.gp[800:800 + s.pr, pl.ds(pl.multiple_of(s.z * s.pc, 128), s.pc)].astype(f32)
+        for j in range(s.nz - 1): t = t + s.v.gp[896:896 + s.pr, j * s.pc:(j + 1) * s.pc].astype(f32)
+        s.v.out[3][...] = t
+    def fsum(s):
+        for j in range(s.nz): s.lf(j).wait()
+        n = s.fh; w = 2 * s.fc
+        for q in range(4):
+            t = s.c(0) * s.v.gp[0:n, q * w:(q + 1) * w].astype(f32)
+            for j in range(1, s.nz): t = t + s.c(7 + j) * s.v.gp[j * n:(j + 1) * n, q * w:(q + 1) * w].astype(f32)
+            s.v.gp[512:512 + n, q * w:(q + 1) * w] = t.astype(bf16)
+        s.start_v(3)
     def mixed(s, w, i):
-        s.sibc(w, i).wait_recv(); s.load(w, i).wait()
-        return s.cs[0, 0:1, 0:1] * s.own[w][i].astype(f32) + s.cs[1, 0:1, 0:1] * s.sb[w][i].astype(f32)
+        if w < 3:
+            pltpu.make_async_copy(s.own(w, i), s.own(w, i), s.v.lsem.at[w * 8 + i]).wait()
+            s.lds(w, i).wait()
+        else:
+            s.sibv(w, i).wait_recv()
+        if w == 3:
+            return s.own(w, i)[...].astype(f32) + s.sb(w, i)[...].astype(f32)
+        ks = (s.d - s.sib + 8) % 8
+        return s.c(0) * s.own(w, i)[...].astype(f32) + s.v.cs[ks, 0:1, 0:1] * s.sb(w, i)[...].astype(f32)
+    def nc(s, src, dst, w, slot, dev): return s.cp(src, dst, "n", w * 13 + slot, (dev, s.z))
+    def ca(s, w): return s.nc(s.half(s.sb(w, 0), 0), s.land(w, "ra"), w, 4, s.xn)
+    def cb(s, w): return s.nc(s.half(s.sb(w, 0), 1), s.land(w, "rb"), w, 5, s.yn)
+    def cx(s, w, h): return s.nc(s.half(s.sb(w, 1), h), s.half(s.land(w, "rx"), h), w, 6 + h, s.xn)
+    def cy(s, w, h): return s.nc(s.half(s.sb(w, 2), h), s.half(s.land(w, "ry"), h), w, 8 + h, s.yn)
     def a(s, w):
-        t = s.sb[w]
-        t[0] = s.mixed(w, 0).astype(t.dtype); s.ca(w).start(); s.cb(w).start()
-        t[1] = s.mixed(w, 1).astype(t.dtype); s.cx(w, 0).start()
-        t[2] = s.mixed(w, 2).astype(t.dtype); s.cy(w, 1).start()
+        def put(i):
+            ref = s.sb(w, i)
+            ref[...] = s.mixed(w, i).astype(ref.dtype)
+        put(0); s.ca(w).start(); s.cb(w).start()
+        put(1); s.cx(w, 0).start()
+        put(2); s.cy(w, 1).start()
     def r(s, w):
         s.ca(w).wait_recv()
-        t = s.half(s.sb[w].at[2], 0)
-        t[...] = (t[...].astype(f32) + s.ra[w][...].astype(f32)).astype(t.dtype)
+        t = s.half(s.sb(w, 2), 0)
+        t[...] = (t[...].astype(f32) + s.land(w, "ra")[...].astype(f32)).astype(t.dtype)
         s.cy(w, 0).start()
         s.cb(w).wait_recv()
-        t = s.half(s.sb[w].at[1], 1)
-        t[...] = (t[...].astype(f32) + s.rb[w][...].astype(f32)).astype(t.dtype)
+        t = s.half(s.sb(w, 1), 1)
+        t[...] = (t[...].astype(f32) + s.land(w, "rb")[...].astype(f32)).astype(t.dtype)
         s.cx(w, 1).start()
     def zpiece(s, w, k):
-        ref = s.zs[w]
-        if w in (0, 1): return ref.at[k]
+        ref = s.land(w, "zs")
+        if w < 2: return ref.at[k]
         if w == 4: return ref
-        if w == 2:
-            r = ref.shape[0] // s.nz
-            return ref.at[pl.ds(pl.multiple_of(k * r, 16), r)]
-        c = ref.shape[1] // s.nz
-        return ref.at[:, pl.ds(pl.multiple_of(k * c, 128), c)]
+        return ref.at[pl.ds(pl.multiple_of(k * s.fh, 16), s.fh)]
+    def zland(s, w, j):
+        if w < 2: return (s.v.zrq, s.v.zro)[w].at[j]
+        if w == 4: return s.v.vs.at[8 + j]
+        return s.v.F.at[pl.ds(s.nz * s.fh + j * s.fh, s.fh), pl.ds(4 * s.fc, s.fc)]
     def zc(s, w, j):
         to = (s.z + j) % s.nz
-        return s.cp(s.zpiece(w, to), s.zr[w].at[j - 1], w, 9 + j, (s.d, to))
+        return s.cp(s.zpiece(w, to), s.zland(w, j - 1), "n", w * 13 + 9 + j, (s.d, to))
     def f(s, w):
         t = s.mixed(w, 3)
         for h in (0, 1):
             s.cx(w, h).wait_recv(); s.cy(w, h).wait_recv()
-        t = t + s.rx[w][...].astype(f32) + s.ry[w][...].astype(f32)
-        if w in (0, 1):
+        t = t + s.land(w, "rx")[...].astype(f32) + s.land(w, "ry")[...].astype(f32)
+        if w == 3:
+            s.v.out[2][0:s.fh, :] = t
+            return
+        ref = s.land(w, "zs")
+        if w < 2:
             c = t.shape[1] // s.nz
-            for k in range(s.nz): s.zs[w][k] = t[:, k * c:(k + 1) * c].astype(bf16)
+            for k in range(s.nz): ref[k] = t[:, k * c:(k + 1) * c].astype(bf16)
         else:
-            s.zs[w][...] = t.astype(s.zs[w].dtype)
+            ref[...] = t.astype(ref.dtype)
         for j in range(1, s.nz): s.zc(w, j).start()
     def zf(s, w):
         for j in range(1, s.nz): s.zc(w, j).wait_recv()
         t = s.zpiece(w, s.z)[...].astype(f32)
-        for j in range(s.nz - 1): t = t + s.zr[w][j].astype(f32)
-        s.out[w][...] = t
-    def finish(s, w):
-        for i in range(4): s.sibc(w, i).wait_send()
-        s.ca(w).wait_send(); s.cb(w).wait_send()
-        for h in (0, 1): s.cx(w, h).wait_send(); s.cy(w, h).wait_send()
-        for j in range(1, s.nz): s.zc(w, j).wait_send()
-
-
-def rs_kernel(c, *refs):
-    refs = list(refs)
-    take = lambda n: [refs.pop(0) for _ in range(n)]
-    grads = take(5); outs = take(5)
-    parts = [take(5) for _ in range(8)]
-    s = Scatter(grads, *parts, outs, *refs)
-    greet(s.partners)
-    q, o, f, p, v = range(5)
-    for w in (o, v, q, f, p): s.s0(w)
-    s.cs[0] = jnp.full(s.cs.shape[1:], c[0], f32)
-    s.cc().start(); s.cc().wait_recv()
-    s.a(o); s.a(v); s.a(q); s.r(o); s.r(v); s.a(f); s.r(q); s.f(o); s.f(v); s.a(p); s.r(f); s.f(q); s.r(p); s.f(f)
-    s.zf(o); s.zf(v); s.zf(q); s.f(p); s.zf(f); s.zf(p)
-    s.cc().wait_send()
-    for w in range(5): s.finish(w)
-
-
-def scatter_all(c, gq, go, gf, gp, gv):
-    nz = lax.axis_size("fsdp")
-    grads = (gq, go, gf, gp, gv)
-    blocks = [(gq.shape[0] // 8, gq.shape[1]), (go.shape[0] // 8, go.shape[1]), (gf.shape[0], gf.shape[1] // 8), (gp.shape[0] // 8, gp.shape[1]), gv.shape[1:]]
-    dt = [bf16] * 4 + [f32]
-    ha = [(split(r), c_) for r, c_ in blocks]
-    hb = [(r - split(r), c_) for r, c_ in blocks]
-    piece = [(r, c_ // nz) for r, c_ in blocks[:2]] + [(blocks[2][0] // nz, blocks[2][1]), (blocks[3][0], blocks[3][1] // nz), blocks[4]]
-    zs = [(nz,) + piece[0], (nz,) + piece[1]] + blocks[2:]
-    zr = [(nz - 1,) + s for s in piece]
-    V = lambda ss: [pltpu.VMEM(s, t) for s, t in zip(ss, dt)]
-    four = [(4,) + b for b in blocks]
-    vm = pl.BlockSpec(memory_space=pltpu.VMEM)
-    an = pl.BlockSpec(memory_space=pl.ANY)
-    dma = pltpu.SemaphoreType.DMA
-    return pl.pallas_call(rs_kernel, out_shape=[jax.ShapeDtypeStruct(s, f32) for s in piece],
-        in_specs=[pl.BlockSpec(memory_space=pltpu.SMEM)] + [an] * 5, out_specs=[vm] * 5,
-        scratch_shapes=V(four) + V(four) + V(ha) + V(hb) + V(blocks) + V(blocks) + V(zs) + V(zr)
-            + [pltpu.VMEM((2, 8, 128), f32), dma((2,)), dma((5, 4)), dma((5, 13)), dma((5, 13))],
-        compiler_params=pltpu.CompilerParams(collective_id=1, has_side_effects=True, vmem_limit_bytes=60 << 20))(c, *grads)
+        for j in range(s.nz - 1): t = t + s.zland(w, j)[...].astype(f32)
+        if w == 2: s.v.out[2][s.fh:, :] = t
+        else: s.v.out[w][...] = t
+    def finish(s):
+        for k in range(1, 8): s.pp(k).wait_send()
+        for j in range(1, s.nz): s.pf(j).wait_send(); s.pz(j).wait_send()
+        for w in range(3):
+            for i in range(4): s.s0all(w, i).wait_send()
+        for i in range(len(s.peers)): s.cc(i).wait_send()
+        for w in range(5):
+            if w > 2:
+                for i in range(4): s.sibv(w, i).wait_send()
+            s.ca(w).wait_send(); s.cb(w).wait_send()
+            for h in (0, 1): s.cx(w, h).wait_send(); s.cy(w, h).wait_send()
+            if w != 3:
+                for j in range(1, s.nz): s.zc(w, j).wait_send()
 
 
 def block_kernel(names, remote, length, tok, cot, *refs):
     refs = list(refs)
     take = lambda n: [refs.pop(0) for _ in range(n)]
     if remote:
-        raw = take(5)
-        y, gx, gq, go, gf, gp, gv, ss = take(8)
+        clip, *raw = take(6)
+        y, gx, ss, *outs = take(8)
+        gq, go, gf, gp, sQ, sO, sF, pP, pF = take(9)
         QT, OT, F, PT, V, sq, so, sf, sp, zq, zo, send, recv = take(13)
+        gv, vs, cs, zrq, zro, lsem, *rsem = take(18)
     else:
         QT, OT, F, PT, vec, bf = take(6)
         y, gx, gq, go, gf, gp, col, dbf, ss = take(9)
@@ -490,6 +580,8 @@
         rows = sq.shape[0]
         items = [(4, 0, 16), (0, 0, rows // 2), (0, rows // 2, rows - rows // 2), (1, 0, so.shape[0]), (2, 0, F.shape[0]), (3, 0, sp.shape[0])]
         g = Gather(items, (sq, so, sf, sp, raw[4]), (zq, zo), (QT, OT, F, PT, V), send, recv)
+        place_of = types.SimpleNamespace(QT=QT, OT=OT, F=F, PT=PT, gp=s.gp, n1=s.n1, A=s.A, gv=gv, vs=vs, cs=cs, zq=zq, zo=zo, zrq=zrq, zro=zro, lsem=lsem, out=outs)
+        red = Reduce((gq, go, gf, gp), (pP, pF), (sQ, sO, sF), place_of, {k: (rsem[2 * i], rsem[2 * i + 1]) for i, k in enumerate("pfsczn")})
         sq[...] = raw[0][...].astype(bf16).T
         so[...] = raw[1][...].astype(bf16).T
         sf[...] = raw[2][...].astype(bf16)
@@ -520,29 +612,49 @@
     ce.wait(); s.ey_mask()
     if remote: g.e4(p)
     s.wgrad(s.ey, s.u, gp, 512, FF)
-    if remote: g.e5(p)
+    if remote: red.start_p(); g.e5(p)
     s.y()
     cy = pltpu.make_async_copy(s.er, y, s.isem.at[2]); cy.start()
-    s.ef(); s.wgrad(s.n2, s.gp, gf, 512, FF); s.gn2()
+    s.ef(); s.wgrad(s.n2, s.gp, gf, 512, FF)
+    if remote: red.start_f(); red.start_s(2)
+    s.gn2()
     cy.wait()
-    s.ln2b(); s.wgrad(s.er, s.A, go, 256, D); s.eA()
+    s.ln2b(); s.wgrad(s.er, s.A, go, 256, D)
+    if remote: red.start_s(1)
+    s.eA()
     loop(D // 128, s.attend_back)
-    s.bias_cols(); s.gn1(); s.ln1b()
+    s.wgrad(s.u, s.n1, gq, 256, D)
+    if remote:
+        for i in range(6): g.finish(i)
+        red.start_s(0); red.load_own(1); red.load_own(2)
+    s.bias_cols(); s.gn1()
+    if remote: red.load_own(0)
+    s.ln1b()
     cg = pltpu.make_async_copy(s.er, gx, s.isem.at[3]); cg.start()
-    s.wgrad(s.u, s.n1, gq, 256, D)
+    norm2 = s.norm()
+    if not remote:
+        ss[0] = norm2
+        cg.wait()
+        col[...] = s.col[...]; dbf[...] = s.dbf[...]
+        return
+    norm = jnp.sqrt(jnp.full((8, 128), norm2, f32))
+    ss[...] = norm
+    w = D // 8; nb = FF // 8 // 128
+    for d in range(8):
+        gv[d, 0:8, 0:w] = s.col[:, d * w:(d + 1) * w]
+        gv[d, 0:8, w:128] = jnp.zeros((8, 128 - w), f32)
+        for j in range(8):
+            k = d * nb + j
+            gv[d, 8 + j:9 + j, :] = s.dbf[:, k * 128:(k + 1) * 128] if j < nb else jnp.zeros((1, 128), f32)
+    red.factors(jnp.minimum(1.0, clip[0] / norm))
+    q, o, f, h, v = range(5)
+    red.load_sib(o); red.load_sib(q); red.load_sib(f); red.load_p(); red.load_f()
+    red.wait_factors()
+    red.start_v(v)
+    red.a(o); red.a(q); red.a(v); red.r(o); red.psum(); red.a(f); red.r(q); red.r(v); red.fsum(); red.f(o); red.f(v); red.r(f); red.a(h); red.f(q)
+    red.r(h); red.zf(o); red.zf(v); red.pfin(); red.f(f); red.f(h); red.zf(q); red.zf(f)
+    red.finish()
     cg.wait()
-    ss[0] = s.norm()
-    if remote:
-        w = D // 8; nb = FF // 8 // 128
-        for d in range(8):
-            gv[d, 0:8, 0:w] = s.col[:, d * w:(d + 1) * w]
-            gv[d, 0:8, w:128] = jnp.zeros((8, 128 - w), f32)
-            for j in range(8):
-                k = d * nb + j
-                gv[d, 8 + j:9 + j, :] = s.dbf[:, k * 128:(k + 1) * 128] if j < nb else jnp.zeros((1, 128), f32)
-        for i in range(6): g.finish(i)
-    else:
-        col[...] = s.col[...]; dbf[...] = s.dbf[...]
 
 
 def run_block(remote, length, tok, cot, *ws):
@@ -553,25 +665,39 @@
     extra = []
     if remote:
         nz = lax.axis_size("fsdp")
-        q, o, f, p, v = ws
+        clip, q, o, f, p, v = ws
         FF = f.shape[1] * 8
         qt, ot, pt = q.shape[::-1], o.shape[::-1], p.shape[::-1]
+        fh = D // nz // 2; fc = FF // 8
         extra = [pltpu.VMEM((3 * D, D), bf16), pltpu.VMEM((D, D), bf16), pltpu.VMEM((D, FF), bf16), pltpu.VMEM((D, FF), bf16), pltpu.VMEM((8,) + v.shape, f32),
             pltpu.VMEM(qt, bf16), pltpu.VMEM(ot, bf16), pltpu.VMEM(f.shape, bf16), pltpu.VMEM(pt, bf16),
-            pltpu.VMEM((nz,) + qt, bf16), pltpu.VMEM((nz,) + ot, bf16), dma((6, 11)), dma((6, 11))]
-        tail = [sd((8,) + v.shape, f32)]
+            pltpu.VMEM((nz,) + qt, bf16), pltpu.VMEM((nz,) + ot, bf16), dma((6, 11)), dma((6, 11)),
+            pltpu.VMEM((8, 16, 128), f32), pltpu.VMEM((12, 16, 128), f32), pltpu.VMEM((8 + nz - 1, 8, 128), f32),
+            pltpu.VMEM((nz - 1,) + qt, bf16), pltpu.VMEM((nz - 1,) + ot, bf16), dma((36,))]
+        for n in (7, 3, 12, 10, 3, 65): extra += [dma((n,)), dma((n,))]
+        outs = [sd((8, 128), f32), sd(qt, f32), sd(ot, f32), sd(f.shape, f32), sd(pt, f32), sd((16, 128), f32)]
+        hbm = [sd((4, 3 * D // 8, D), bf16), sd((4, D // 8, D), bf16), sd((4, nz * fh, fc), bf16), sd((7, D // 8, FF), bf16), sd((nz - 1, fh, FF), bf16)]
+        ins = [sm] + [vm] * 5
     else:
         FF = ws[2].shape[1]
-        tail = [sd((8, D), f32), sd((1, FF), f32)]
+        outs, hbm = [], []
+        ins = [vm] * len(ws)
+    acts = [sd((L, D), bf16), sd((L, D), bf16)]
+    grads = [sd((3 * D, D), bf16), sd((D, D), bf16), sd((D, FF), bf16), sd((D, FF), bf16)]
     scr = scratch(L, D, FF)
     params = dict(collective_id=0, has_side_effects=True) if remote else {}
-    return pl.pallas_call(functools.partial(block_kernel, list(scr), remote),
-        out_shape=[sd((L, D), bf16), sd((L, D), bf16), sd((3 * D, D), bf16), sd((D, D), bf16), sd((D, FF), bf16), sd((D, FF), bf16)] + tail + [sd((1,), f32)],
-        in_specs=[sm, an, an] + [vm] * len(ws), out_specs=[an] * 6 + [vm] * len(tail) + [sm], scratch_shapes=extra + list(scr.values()),
+    if remote:
+        shapes = acts + outs + grads + hbm
+        specs = [an] * 2 + [vm] * 6 + [an] * 9
+    else:
+        shapes = acts + grads + [sd((8, D), f32), sd((1, FF), f32), sd((1,), f32)]
+        specs = [an] * 6 + [vm, vm, sm]
+    return pl.pallas_call(functools.partial(block_kernel, list(scr), remote), out_shape=shapes,
+        in_specs=[sm, an, an] + ins, out_specs=specs, scratch_shapes=extra + list(scr.values()),
         compiler_params=pltpu.CompilerParams(vmem_limit_bytes=VLIM, **params))(length, tok, cot, *ws)
 
 
-VLIM = 63 << 20
+VLIM = (63 << 20) + (768 << 10)
 
 
 def shards(tokens, qkv_weight, out_weight, fc_weight, proj_weight, fc_bias, vectors, cotangent, lengths, clip_norm,
@@ -580,18 +706,16 @@
     if ndp == 8:
         nb = fc_bias.shape[0] // 128
         small = jnp.concatenate([jnp.pad(vectors, ((0, 0), (0, 128 - vectors.shape[1]))), jnp.pad(fc_bias.reshape(nb, 128), ((0, 8 - nb), (0, 0)))], axis=0)
-        y, gx, gq, go, gf, gp, gv, ss = run_block(True, lengths, tokens, cotangent, qkv_weight, out_weight, fc_weight, proj_weight, small)
+        y, gx, norm, sq, so, sf, sp, sv, *_ = run_block(True, lengths, tokens, cotangent, clip_norm.reshape(1), qkv_weight, out_weight, fc_weight, proj_weight, small)
+        norm = norm[0, :1]
+        finals = (sq.T, so.T, sf, sp.T, sv[8:8 + nb].reshape(-1), sv[:8, :vectors.shape[1]])
     else:
         g = lambda a: lax.all_gather(lax.all_gather(a.astype(bf16), "dp", axis=1, tiled=True), "fsdp", axis=0, tiled=True)
         vec = lax.all_gather(vectors.astype(bf16), "dp", axis=1, tiled=True).astype(f32)
         bf = lax.all_gather(fc_bias.astype(bf16), "dp", axis=0, tiled=True).astype(f32).reshape(1, -1)
         y, gx, gq, go, gf, gp, col, dbf, ss = run_block(False, lengths, tokens, cotangent, g(qkv_weight).T, g(out_weight).T, g(fc_weight), g(proj_weight).T, vec, bf)
-    norm = jnp.sqrt(ss)
-    factor = jnp.minimum(1.0, clip_norm / norm)
-    if ndp == 8:
-        sq, so, sf, sp, sv = scatter_all(factor, gq, go, gf, gp, gv)
-        finals = (sq.T, so.T, sf, sp.T, sv[8:8 + nb].reshape(-1), sv[:8, :vectors.shape[1]])
-    else:
+        norm = jnp.sqrt(ss)
+        factor = jnp.minimum(1.0, clip_norm / norm)
         ps = lambda a, dim: lax.psum_scatter(factor * a.astype(f32), "dp", scatter_dimension=dim, tiled=True)
         pz = lambda a: lax.psum_scatter(a.astype(bf16), "fsdp", scatter_dimension=0, tiled=True).astype(f32)
         finals = tuple(pz(ps(a, 1)) for a in (gq.T, go.T, gf, gp.T)) + lax.psum((ps(dbf[0], 0), ps(col, 1)), "fsdp")

time: 286 us -> 256 us (0.90)
  Pallas kernels: 269 us -> 236 us
    pallas_call x1 -> x0, Pallas kernels: 86.7 us -> none  [scatter_all(): pl.pallas_call(rs_kernel, out_shape=[jax.ShapeDtypeStruct(s, f32) for s i...]
    pallas_call x1, Pallas kernels: 182 us -> 236 us  [run_block(): pl.pallas_call(functools.partial(block_kernel, list(scr), remote), out_sh...]
    unnamed x29 -> x27, local copies, waits for them, and re-layouts: 6.87 us -> 7.87 us
where the time goes in v3:
time: 256 us; the launch traced here: 255 us
  Pallas kernels  236 us (92%)
  local copies, waits for them, and re-layouts  9.06 us (4%)
  other arithmetic  6.47 us (3%)
  between operations  3.86 us (2%)
    pallas_call x1, Pallas kernels, run_block(): pl.pallas_call(functools.partial(block_kernel, list(scr), remote), out_sh...  236 us
    unnamed x27, local copies, waits for them, and re-layouts  7.87 us
    add x6, other arithmetic, shards(): a / examples + n  5.16 us

profile of v3, /device:TPU:0, one launch (start us, length us, event | category | flops | bytes accessed | tf_op | source)
XLA Modules:
  0.0 255.2 jit_solution(1836862076893080513)
XLA Ops:
  1.3 1.9 copy.25.refs_4_
  3.2 1.3 select_maximum_fusion.refs_5_
  5.1 0.0 copy-start.8
  5.1 0.0 copy-start.9
  5.1 235.8 %shard_map.223 = (bf16[1024,768]{1,0:T(8,128)(2,1)}, bf16[1024,768]{1,0:T(8,128)(2,1)}, f32[8,128]{1,0:T(8,128)}, f32[288,192]{1,0:T(8,128)}, f32[96,192]{1,0:T(...) custom-call(s32[1]{0:T(128)S(6)} %copy.32.length, ...), custom_call_target="tpu_custom_call" | custom-call | tf_op jit(solution)/shard_map/pallas_call | solution.py:695
  241.0 0.0 copy-start.2
  241.0 0.0 copy-start.5
  241.0 0.0 copy-start.6
  241.0 0.0 copy-done.8
  241.0 1.3 multiply_add_fusion.1
  242.4 0.0 copy-done.9
  242.4 1.3 bitcast_add_fusion.3
  243.6 1.2 slice.9
  245.5 0.0 copy-start.7
  245.5 1.1 copy.26
  246.6 0.0 copy-start.3
  246.7 0.0 copy-start.4
  246.7 1.1 bitcast_add_fusion.1
  247.7 0.0 copy-start.1
  247.7 0.9 copy.28
  248.6 0.0 copy-done.2
  248.6 0.0 copy-done.5
  248.6 0.7 bitcast_add_fusion
  249.4 0.0 copy-done.6
  249.4 0.1 copy.27
  249.5 0.0 copy-done.7
  249.5 0.7 copy.29
  250.2 0.0 copy-done.3
  250.2 0.0 copy-done.4
  250.2 0.7 multiply_add_fusion
  251.0 0.0 copy-done.1
  251.0 0.0 copy-start
  251.0 1.1 copy.34
  252.1 0.8 copy-done
  253.0 1.1 copy.35
  (1 shorter events, 0.0 us)
Async XLA Ops:
  5.1 235.9 %copy-start.8 = (f32[8,96]{1,0:T(8,128)S(1)}, f32[8,96]{1,0:T(8,128)}, u32[]{:S(2)}) copy-start(f32[8,96]{1,0:T(8,128)} %param.31) | copy-start | bytes 9220
  5.1 237.2 %copy-start.9 = (f32[384]{0:T(512)S(1)}, f32[384]{0:T(512)}, u32[]{:S(2)}) copy-start(f32[384]{0:T(512)} %param.30) | copy-start | bytes 4612
  241.0 7.6 %copy-start.2 = (f32[768,96]{0,1:T(8,128)S(1)}, f32[768,96]{0,1:T(8,128)}, u32[]{:S(2)}) copy-start(f32[768,96]{0,1:T(8,128)} %param.29) | copy-start | bytes 884740
  241.0 7.6 %copy-start.5 = (f32[96,768]{1,0:T(8,128)S(1)}, f32[96,768]{1,0:T(8,128)}, u32[]{:S(2)}) copy-start(f32[96,768]{1,0:T(8,128)} %get-tuple-element.23) | copy-start | bytes 884740
  241.0 8.3 %copy-start.6 = (f32[192,96]{1,0:T(8,128)S(1)}, f32[192,96]{1,0:T(8,128)}, u32[]{:S(2)}) copy-start(f32[192,96]{1,0:T(8,128)} %param.27) | copy-start | bytes 221188
  245.5 4.0 %copy-start.7 = (f32[96,192]{1,0:T(8,128)S(1)}, f32[96,192]{1,0:T(8,128)}, u32[]{:S(2)}) copy-start(f32[96,192]{1,0:T(8,128)} %get-tuple-element.21) | copy-start | bytes 221188
  246.6 3.6 %copy-start.3 = (f32[192,384]{1,0:T(8,128)S(1)}, f32[192,384]{1,0:T(8,128)}, u32[]{:S(2)}) copy-start(f32[192,384]{1,0:T(8,128)} %param.28) | copy-start | bytes 884740
  246.7 3.6 %copy-start.4 = (f32[192,384]{1,0:T(8,128)S(1)}, f32[192,384]{1,0:T(8,128)}, u32[]{:S(2)}) copy-start(f32[192,384]{1,0:T(8,128)} %get-tuple-element.22) | copy-start | bytes 884740
  247.7 3.2 %copy-start.1 = (bf16[1024,768]{1,0:T(8,128)(2,1)S(1)}, bf16[1024,768]{1,0:T(8,128)(2,1)}, u32[]{:S(2)}) copy-start(bf16[1024,768]{1,0:T(8,128)(2,1)} %get-tuple-element.43) | copy-start | bytes 4718596
  251.0 2.0 copy-start
